TPU v7x, 32 devices: a whole 2x2x4 slice. The times are simulated.
32 devices in a mesh: dp: 8 (over y, x, core), ctx: 4 (over z).
Axes of the slice: x: 2, y: 2, z: 4, core: 2. Of those that a mesh axis runs over, the one named last changes fastest.
Arguments:
- tokens: bfloat16 [8192, 4096], P(('dp', 'ctx')), may hold values from -28 to 28
- projection: bfloat16 [4096, 3072], P('dp'), may hold values from -0.09375 to 0.09375
- placement: int32 [32, 32], P(('dp', 'ctx')), may hold values from 0 to 31, each once within a row
- doc_lengths: int32 [8, 8], P('dp'), may hold values from 1 to 512, 1024 in all within a row
Outputs:
- attended: bfloat16 [8192, 2048], P(('dp', 'ctx'))
Inputs may be any that keep to these rules, and one draw needn't show every extreme that they name: `placement`: row i lists for each of the 8-row pieces of loader block i the device that computes it; every device appears once in each row. `doc_lengths`: each row holds the documents of one packed sequence of 1024 tokens in order, one of exactly 512 tokens.
All inputs are finite; a program needn't handle non-finite values.
Results may differ from a plain program's by a relative error of at most 0.006.
The roundings to bfloat16 on the way count: a program that leaves them out, or rounds other values in their place, can miss the bound.
Values may be sent and summed in bfloat16 or wider, within the bound.
A program may use at most 128 MiB of HBM per device.

v0:
```python
import jax
import jax.numpy as jnp
from jax import lax
from jax.sharding import PartitionSpec as P

HEAD_DIM = 128
HEADS = 16
KV_HEADS = 4


theta_base = 500000.0


def doc_tables(lengths, position):
    doc_ends = jnp.cumsum(lengths)
    doc_starts = doc_ends - lengths
    segment = jnp.sum((position[:, None] >= doc_ends[None, :]).astype(jnp.int32), axis=1)
    one_hot = segment[:, None] == jnp.arange(lengths.shape[0], dtype=jnp.int32)[None, :]
    begins = jnp.sum(jnp.where(one_hot, doc_starts[None, :], 0), axis=1)
    return (segment, position - begins)


def rotate(values, offsets, head_count):
    row_count = values.shape[0]
    half_dim = HEAD_DIM // 2
    frequency = theta_base ** (-2.0 * jnp.arange(half_dim, dtype=jnp.float32) / HEAD_DIM)
    angles = offsets.astype(jnp.float32)[:, None] * frequency[None, :]
    cosine = jnp.cos(angles)[:, None, :]
    sine = jnp.sin(angles)[:, None, :]
    halves = values.astype(jnp.float32).reshape(row_count, head_count, 2, half_dim)
    former = halves[:, :, 0]
    latter = halves[:, :, 1]
    result = jnp.stack([former * cosine - latter * sine, latter * cosine + former * sine], axis=2)
    return result.reshape(row_count, head_count * HEAD_DIM).astype(jnp.bfloat16)


def on_device(tokens, projection, placement, doc_lengths):
    row_count = tokens.shape[0]
    dev_count = placement.shape[1]
    piece_rows = row_count // dev_count
    destinations = placement[0]
    slot_of = (
        jnp.zeros((dev_count,), jnp.int32)
        .at[destinations]
        .set(jnp.arange(dev_count, dtype=jnp.int32))
    )
    outgoing = tokens.reshape(dev_count, piece_rows, tokens.shape[1])[slot_of]
    arrived = lax.all_to_all(
        outgoing, ("dp", "ctx"), split_axis=0, concat_axis=0, tiled=True
    ).reshape(row_count, tokens.shape[1])
    summed = jnp.dot(
        arrived,
        lax.all_gather(projection, "dp", axis=0, tiled=True),
        preferred_element_type=jnp.float32,
    )
    projected = summed.astype(jnp.bfloat16)
    lengths = doc_lengths[0]
    position = lax.axis_index("ctx") * row_count + jnp.arange(row_count, dtype=jnp.int32)
    segment, offsets = doc_tables(lengths, position)
    query_width = HEADS * HEAD_DIM
    key_width = KV_HEADS * HEAD_DIM
    queries = rotate(projected[:, :query_width], offsets, HEADS)
    key_rows = rotate(projected[:, query_width : query_width + key_width], offsets, KV_HEADS)
    value_rows = projected[:, query_width + key_width :]
    group_size = HEADS // KV_HEADS
    query_major = jnp.transpose(
        queries.reshape(row_count, KV_HEADS, group_size, HEAD_DIM), (1, 0, 2, 3)
    )
    score_scale = HEAD_DIM ** (-0.5)
    key_block = lax.all_gather(key_rows, "ctx", axis=0, tiled=True)
    value_block = lax.all_gather(value_rows, "ctx", axis=0, tiled=True)
    key_count = key_block.shape[0]
    key_index = jnp.arange(key_count, dtype=jnp.int32)
    key_segment, unused = doc_tables(lengths, key_index)
    allowed = (segment[:, None] == key_segment[None, :]) & (key_index[None, :] <= position[:, None])
    key_major = jnp.transpose(key_block.reshape(key_count, KV_HEADS, HEAD_DIM), (1, 0, 2))
    value_major = jnp.transpose(value_block.reshape(key_count, KV_HEADS, HEAD_DIM), (1, 0, 2))

    def per_head(inputs):
        query_head, key_head, value_head, row_max, row_sum, weighted = inputs
        scores = (
            jnp.einsum("tgd,sd->tgs", query_head, key_head, preferred_element_type=jnp.float32)
            * score_scale
        )
        scores = jnp.where(allowed[:, None, :], scores, -jnp.inf)
        new_max = jnp.maximum(row_max, jnp.max(scores, axis=-1))
        factor = jnp.exp(row_max - new_max)
        weights = jnp.exp(scores - new_max[..., None])
        row_sum = row_sum * factor + jnp.sum(weights, axis=-1)
        weighted = weighted * factor[..., None] + jnp.einsum(
            "tgs,sd->tgd",
            weights.astype(jnp.bfloat16),
            value_head,
            preferred_element_type=jnp.float32,
        )
        return (new_max, row_sum, weighted)

    row_max = jnp.full((KV_HEADS, row_count, group_size), -1e30, jnp.float32)
    row_sum = jnp.zeros((KV_HEADS, row_count, group_size), jnp.float32)
    weighted = jnp.zeros((KV_HEADS, row_count, group_size, HEAD_DIM), jnp.float32)
    row_max, row_sum, weighted = lax.map(
        per_head, (query_major, key_major, value_major, row_max, row_sum, weighted)
    )
    mixed = (
        jnp.transpose(weighted / row_sum[..., None], (1, 0, 2, 3))
        .reshape(row_count, query_width)
        .astype(jnp.bfloat16)
    )
    returned = lax.all_to_all(
        mixed.reshape(dev_count, piece_rows, query_width),
        ("dp", "ctx"),
        split_axis=0,
        concat_axis=0,
        tiled=True,
    )
    return returned[destinations].reshape(row_count, query_width)


def solution(mesh):
    return jax.shard_map(
        on_device,
        mesh=mesh,
        in_specs=(P(("dp", "ctx"), None), P("dp", None), P(("dp", "ctx"), None), P("dp", None)),
        out_specs=P(("dp", "ctx"), None),
        check_vma=False,
    )
```

profile of v0, /device:TPU:0, one launch (start us, length us, event | category | flops | bytes accessed | tf_op | source)
XLA Modules:
  0.0 294.8 jit_solution(10143432318603384629)
XLA Ops:
  8.1 2.0 gather_fusion
  10.1 54.9 %all_to_all.10 = bf16[32,8,4096]{2,1,0:T(8,128)(2,1)} all-to-all(bf16[32,8,4096]{2,1,0:T(8,128)(2,1)} %gather_fusion), channel_id=1, replica_groups=mesh['dp'=8,'ctx'=4] {'dp','ctx'}, dimensions={0} | all-to-all | bytes 4194304 | tf_op jit(solution)/shard_map/all_to_all | solution.py:48
  65.1 89.7 %all-gather.4.cloned.1.call-done = bf16[4096,3072]{1,0:T(8,128)(2,1)} async-done(((bf16[512,3072]{1,0:T(8,128)(2,1)}), bf16[4096,3072]{1,0:T(8,128)(2,1)}) %all-gather.4.cloned.1.call-update) | async-done | bytes 25165840 | tf_op jit(solution)/shard_map/all_gather | solution.py:53
  154.7 12.2 %convolution_convert_fusion = bf16[256,3072]{1,0:T(8,128)(2,1)S(1)} fusion(bf16[4096,3072]{1,0:T(8,128)(2,1)} %all-gather.4.cloned.1.call-done, bf16[32,8,4096]{2,1,0:T(8,128)(2,1)} %all_to_all.10), kind=kOutput, calls=%fused_computation.30 | convolution fusion | flops 6443237376 | bytes 28835840 | tf_op jit(solution)/shard_map/dot_general | solution.py:51
  170.8 2.8 slice_convert_fusion
  173.6 2.9 copy.13
  176.5 1.9 subtract_convert_fusion
  178.6 18.4 %all-gather.8.cloned.1.call-done = bf16[1024,512]{1,0:T(8,128)(2,1)} async-done(((bf16[256,512]{1,0:T(8,128)(2,1)}), bf16[1024,512]{1,0:T(8,128)(2,1)}) %all-gather.8.cloned.1.call-update) | async-done | bytes 1048592 | tf_op jit(solution)/shard_map/all_gather | solution.py:71
  197.0 2.4 bitcast_bitcast_fusion
  199.4 28.9 %all-gather.6.cloned.1.call-done = bf16[1024,512]{0,1:T(8,128)(2,1)} async-done(((bf16[256,512]{0,1:T(8,128)(2,1)}), bf16[1024,512]{0,1:T(8,128)(2,1)}) %all-gather.6.cloned.1.call-update) | async-done | bytes 1048592 | tf_op jit(solution)/shard_map/all_gather | solution.py:70
  228.3 26.0 %while.13 = (s32[]{:T(128)}, f32[4,256,4]{1,2,0:T(4,128)S(1)}, f32[4,256,4,128]{3,1,2,0:T(8,128)}, bf16[4,256,4,128]{1,3,2,0:T(8,128)(2,1)S(1)}, bf16[4,1024,128...) while((s32[]{:T(128)}, f32[4,256,4]{1,2,0:T(4,128)S(1)}, ...), condition=%wide.region_8.9_spmd.clone, body=%wide.region_5.8_spmd.clone.sunk | while | flops 549327872 | bytes 14995561 | solution.py:101
  228.6 1.9 fusion.47
  230.6 3.0 %fusion.49 = f32[4,256,4,128]{3,1,2,0:T(8,128)} fusion(f32[4,256,4,128]{3,1,2,0:T(8,128)} %get-tuple-element.191, s32[]{:T(128)} %get-tuple-element.189, f32[256,4,1024]{2,0,1:T(8,128)S(1)} %get-tuple-element.175, f32[256,4]{0,1:T(4,128)S(1)} %get-tuple-element.177, pred[256,1024]{1,0:T(8,128)(4,1)S(1)} %fusion.46, ...), kind=kOutput, calls=%fused_computation.13.clone.1 | convolution fusion | flops 272760832 | bytes 5252096 | tf_op jit(solution)/shard_map/while/body/eval_jaxpr/tgs,sd->tgd/dot_general | solution.py:90
  235.2 1.9 fusion.47
  237.1 3.0 %fusion.49 = f32[4,256,4,128]{3,1,2,0:T(8,128)} fusion(f32[4,256,4,128]{3,1,2,0:T(8,128)} %get-tuple-element.191, s32[]{:T(128)} %get-tuple-element.189, f32[256,4,1024]{2,0,1:T(8,128)S(1)} %get-tuple-element.175, f32[256,4]{0,1:T(4,128)S(1)} %get-tuple-element.177, pred[256,1024]{1,0:T(8,128)(4,1)S(1)} %fusion.46, ...), kind=kOutput, calls=%fused_computation.13.clone.1 | convolution fusion | flops 272760832 | bytes 5252096 | tf_op jit(solution)/shard_map/while/body/eval_jaxpr/tgs,sd->tgd/dot_general | solution.py:90
  241.7 1.9 fusion.47
  243.6 3.0 %fusion.49 = f32[4,256,4,128]{3,1,2,0:T(8,128)} fusion(f32[4,256,4,128]{3,1,2,0:T(8,128)} %get-tuple-element.191, s32[]{:T(128)} %get-tuple-element.189, f32[256,4,1024]{2,0,1:T(8,128)S(1)} %get-tuple-element.175, f32[256,4]{0,1:T(4,128)S(1)} %get-tuple-element.177, pred[256,1024]{1,0:T(8,128)(4,1)S(1)} %fusion.46, ...), kind=kOutput, calls=%fused_computation.13.clone.1 | convolution fusion | flops 272760832 | bytes 5252096 | tf_op jit(solution)/shard_map/while/body/eval_jaxpr/tgs,sd->tgd/dot_general | solution.py:90
  248.2 1.9 fusion.47
  250.1 3.0 %fusion.49 = f32[4,256,4,128]{3,1,2,0:T(8,128)} fusion(f32[4,256,4,128]{3,1,2,0:T(8,128)} %get-tuple-element.191, s32[]{:T(128)} %get-tuple-element.189, f32[256,4,1024]{2,0,1:T(8,128)S(1)} %get-tuple-element.175, f32[256,4]{0,1:T(4,128)S(1)} %get-tuple-element.177, pred[256,1024]{1,0:T(8,128)(4,1)S(1)} %fusion.46, ...), kind=kOutput, calls=%fused_computation.13.clone.1 | convolution fusion | flops 272760832 | bytes 5252096 | tf_op jit(solution)/shard_map/while/body/eval_jaxpr/tgs,sd->tgd/dot_general | solution.py:90
  254.3 1.9 fusion.30
  257.1 1.6 convert_element_type.49
  258.7 2.9 all-to-all-start.1
  261.6 25.0 %all-to-all-done.1 = bf16[32,8,2048]{2,1,0:T(8,128)(2,1)S(1)} async-done(((bf16[32,8,2048]{2,1,0:T(8,128)(2,1)}), bf16[32,8,2048]{2,1,0:T(8,128)(2,1)S(1)}, u32[]{:S(2)}, u32[]{:S(2)}) %all-to-all-start.1) | async-done | bytes 1048608 | tf_op jit(solution)/shard_map/all_to_all | solution.py:109
  286.7 1.6 gather_fusion.1
  (53 shorter events, 12.8 us)
Async XLA Ops:
  6.5 1.6 copy-start
  6.5 0.8 copy-start.2
  6.5 148.2 %all-gather.4.cloned.1.call-start = ((), (), s32[]{:S(2)}) async-start(), calls=%async_computation.2 | async-start | bytes 28311552 | tf_op jit(solution)/shard_map/all_gather | solution.py:53
  7.3 189.7 %all-gather.8.cloned.1.call-start = ((), (), s32[]{:S(2)}) async-start(), calls=%async_computation.4 | async-start | bytes 1310720 | tf_op jit(solution)/shard_map/all_gather | solution.py:71
  65.1 103.9 %copy-start.3 = (s32[1,8]{1,0:T(1,128)S(1)}, s32[1,8]{1,0:T(1,128)}, u32[]{:S(2)}) copy-start(s32[1,8]{1,0:T(1,128)} %param.9) | copy-start | bytes 100
  166.9 1.2 copy-start.1
  168.9 59.4 %all-gather.6.cloned.1.call-start = ((), (), s32[]{:S(2)}) async-start(), calls=%async_computation.3 | async-start | bytes 1310720 | tf_op jit(solution)/shard_map/all_gather | solution.py:70
  258.7 28.0 %all-to-all-start.1 = ((bf16[32,8,2048]{2,1,0:T(8,128)(2,1)}), bf16[32,8,2048]{2,1,0:T(8,128)(2,1)S(1)}, u32[]{:S(2)}, u32[]{:S(2)}) async-start(bf16[32,8,2048]{2,1,0:T(8,128)(2,1)} %convert_element_type.49), calls=%async_computation.1 | async-start | bytes 2097152 | tf_op jit(solution)/shard_map/all_to_all | solution.py:109
Sparse Core Ops, SparseCore 0:
  9.2 145.4 all-gather.3
  169.0 27.9 all-gather.7
  198.5 29.6 all-gather.5
where the time goes:
time: 297 us; the launch traced here: 295 us
  waiting for transfers between devices  163 us (55%)
  blocking collectives  54.9 us (18%)
  matrix products  31.7 us (11%)
  other arithmetic  15.6 us (5%)
  local copies, waits for them, and re-layouts  13.5 us (5%)
  between operations  13.3 us (4%)
  starting transfers between devices  2.99 us (1%)
    all_gather x1, waiting for transfers between devices, on_device(): lax.all_gather(projection, 'dp', axis=0, tiled=True)  89.7 us
    all_to_all x1, blocking collectives, on_device(): lax.all_to_all(outgoing, ('dp', 'ctx'), split_axis=0, concat_axis=0, tile...  54.9 us
    all_gather x1, waiting for transfers between devices, on_device(): key_block = lax.all_gather(key_rows, 'ctx', axis=0, tiled=True)  28.9 us
    all_to_all x1, waiting for transfers between devices, on_device(): lax.all_to_all(mixed.reshape(dev_count, piece_rows, query_width), ('dp',...  25 us
    all_gather x1, waiting for transfers between devices, on_device(): value_block = lax.all_gather(value_rows, 'ctx', axis=0, tiled=True)  18.4 us
    dot_general x1, matrix products, on_device(): jnp.dot(arrived, lax.all_gather(projection, 'dp', axis=0, tiled=True), pr...  12.2 us
    dot_general x4, matrix products, per_head(): jnp.einsum('tgs,sd->tgd', weights.astype(jnp.bfloat16), value_head, prefe...  11.9 us
    dot_general x4, matrix products, per_head(): jnp.einsum('tgd,sd->tgs', query_head, key_head, preferred_element_type=jn...  7.58 us
  transfers between devices with their start and end apart: 4, of which 4 were waited for; matrix products, arithmetic and copies ran while one was open for 5% of the time, Pallas kernels for 0%

commit v1 on v0

v1 whole, which is shorter than its diff:
```python
import functools
import math

import jax
import jax.numpy as jnp
from jax import lax
from jax.experimental import pallas as pl
from jax.experimental.pallas import tpu as pltpu
from jax.sharding import PartitionSpec as P

HEAD_DIM = 128
HEADS = 16
KV_HEADS = 4
GROUP = HEADS // KV_HEADS
Q_W = GROUP * HEAD_DIM
PART_W = Q_W + 2 * HEAD_DIM
MOST = 512
MESH = pl.DeviceIdType.MESH

theta_base = 500000.0


def position_tables(lengths, seq):
    position = jnp.arange(seq, dtype=jnp.int32)
    ends = jnp.cumsum(lengths)
    begins = jnp.max(
        jnp.where(position[:, None] >= ends[None, :], ends[None, :], 0), axis=1
    )
    half = HEAD_DIM // 2
    frequency = theta_base ** (-2.0 * jnp.arange(half, dtype=jnp.float32) / HEAD_DIM)
    angles = (position - begins).astype(jnp.float32)[:, None] * frequency[None, :]
    cosine, sine = jnp.cos(angles), jnp.sin(angles)
    return (
        jnp.concatenate([cosine, cosine], axis=1),
        jnp.concatenate([-sine, sine], axis=1),
        jnp.broadcast_to(begins[:, None], (seq, HEAD_DIM)),
    )


def attention_kernel(block, proj_ref, cos_ref, sin_ref, begin_ref, out_ref, key_ref):
    seq = proj_ref.shape[0]
    factor = HEAD_DIM**-0.5 * math.log2(math.e)

    def rotated(rows, column):
        x = proj_ref[rows, column : column + HEAD_DIM].astype(jnp.float32)
        turned = pltpu.roll(x, HEAD_DIM // 2, 1)
        return (x * cos_ref[rows, :] + turned * sin_ref[rows, :]).astype(jnp.bfloat16)

    for b in range(seq // block):
        rows = slice(b * block, (b + 1) * block)
        key_ref[rows, :] = rotated(rows, Q_W)
    for b in range(seq // block):
        rows = slice(b * block, (b + 1) * block)
        first = max(0, (b * block - (MOST - 1)) // block * block)
        keys = slice(first, (b + 1) * block)
        width = (b + 1) * block - first
        at = first + lax.broadcasted_iota(jnp.int32, (block, width), 1)
        own = b * block + lax.broadcasted_iota(jnp.int32, (block, width), 0)
        allowed = (at >= begin_ref[rows, 0:1]) & (at <= own)
        values = proj_ref[keys, Q_W + HEAD_DIM : PART_W]
        for h in range(GROUP):
            scores = lax.dot_general(
                rotated(rows, h * HEAD_DIM),
                key_ref[keys, :],
                (((1,), (1,)), ((), ())),
                preferred_element_type=jnp.float32,
            )
            scores = jnp.where(allowed, scores, -jnp.inf)
            top = jnp.max(scores, axis=1, keepdims=True)
            weights = jnp.exp2((scores - top) * factor)
            total = jnp.sum(weights, axis=1, keepdims=True)
            mixed = jnp.dot(
                weights.astype(jnp.bfloat16), values, preferred_element_type=jnp.float32
            )
            out_ref[rows, h * HEAD_DIM : (h + 1) * HEAD_DIM] = (mixed / total).astype(jnp.bfloat16)


def attention(projected, lengths):
    seq = projected.shape[0]
    cosine, sine, begins = position_tables(lengths, seq)
    return pl.pallas_call(
        functools.partial(attention_kernel, 256),
        out_shape=jax.ShapeDtypeStruct((seq, Q_W), jnp.bfloat16),
        in_specs=[pl.BlockSpec(memory_space=pltpu.VMEM)] * 4,
        out_specs=pl.BlockSpec(memory_space=pltpu.VMEM),
        scratch_shapes=[pltpu.VMEM((seq, HEAD_DIM), jnp.bfloat16)],
        compiler_params=pltpu.CompilerParams(vmem_limit_bytes=32 * 2**20),
    )(projected, cosine, sine, begins)


def gather_kernel(dp, ctx, chunk, tok_ref, w_ref, out_ref, x_ref, w_buf, acc_ref,
                  own_sem, wown_sem, tok_send, tok_recv, z_send, z_recv, c_send, c_recv, w_send, w_recv):
    d, c = lax.axis_index("dp"), lax.axis_index("ctx")
    dc, cz = d % 2, c % 2
    groups = dp * ctx // 4
    halves = ctx // 2
    s_me = (d // 2) * halves + c // 2
    m_me = dc * 2 + cz
    m_z = dc * 2 + 1 - cz
    d_sib, c_sib = d + 1 - 2 * dc, c + 1 - 2 * cz
    slab = groups * chunk
    depth = w_ref.shape[0]

    def class_peer(s):
        return ((s // halves) * 2 + dc, (s % halves) * 2 + cz)

    barrier = pltpu.get_barrier_semaphore()
    met = 0
    for t in range(1, groups):
        pl.semaphore_signal(barrier, inc=1, device_id=class_peer((s_me + t) % groups), device_id_type=MESH)
        met += 1
    for t in range(dp // 2):
        other = ((d // 2 + t) % (dp // 2)) * 2 + 1 - dc
        pl.semaphore_signal(barrier, inc=1, device_id=(other, c), device_id_type=MESH)
        met += 1
    pl.semaphore_signal(barrier, inc=1, device_id=(d, c_sib), device_id_type=MESH)
    pl.semaphore_wait(barrier, met + 1)

    def x_rows(m, s):
        return x_ref.at[pl.ds(pl.multiple_of(m * slab + s * chunk, chunk), chunk), :]

    def tok_rows(s):
        return tok_ref.at[pl.ds(pl.multiple_of(s * chunk, chunk), chunk), :]

    def remote(src, dst, send, recv, device):
        return pltpu.make_async_remote_copy(
            src_ref=src, dst_ref=dst, send_sem=send, recv_sem=recv, device_id=device, device_id_type=MESH
        )

    own = pltpu.make_async_copy(tok_rows(s_me), x_rows(m_me, s_me), own_sem)
    own.start()

    def tok_copy(t):
        s = (s_me + t) % groups
        return remote(tok_rows(s), x_rows(m_me, s_me), tok_send.at[t], tok_recv.at[t], class_peer(s))

    for t in range(1, groups):
        tok_copy(t).start()

    parts = ((0, 0, Q_W), (HEADS * HEAD_DIM, Q_W, HEAD_DIM),
             ((HEADS + KV_HEADS) * HEAD_DIM, Q_W + HEAD_DIM, HEAD_DIM))

    def w_pieces(d_to, d_from):
        g = (d_to % 2) * 2 + cz
        for base, to, width in parts:
            yield (w_ref.at[:, pl.ds(pl.multiple_of(base + g * width, HEAD_DIM), width)],
                   w_buf.at[d_from, :, to : to + width])

    def w_copies(t):
        d_to = (d + t) % dp
        return [remote(src, dst, w_send.at[t, i], w_recv.at[t, i], (d_to, c))
                for i, (src, dst) in enumerate(w_pieces(d_to, d))]

    w_own = [pltpu.make_async_copy(src, dst, wown_sem.at[i]) for i, (src, dst) in enumerate(w_pieces(d, d))]
    for copy in w_own:
        copy.start()
    for t in range(1, dp):
        for copy in w_copies(t):
            copy.start()

    def z_copy(t):
        s = (s_me - t + groups) % groups
        return remote(x_rows(m_me, s), x_rows(m_me, s), z_send.at[t], z_recv.at[t], (d, c_sib))

    def z_arrival(t):
        s = (s_me - t + groups) % groups
        return remote(x_rows(m_z, s), x_rows(m_z, s), z_send.at[t], z_recv.at[t], (d, c_sib))

    def c_copy(which, t):
        s = (s_me - t + groups) % groups
        m = m_me if which == 0 else m_z
        return remote(x_rows(m, s), x_rows(m, s), c_send.at[which, t], c_recv.at[which, t], (d_sib, c))

    def c_arrival(which, t):
        s = (s_me - t + groups) % groups
        m = (1 - dc) * 2 + (cz if which == 0 else 1 - cz)
        return remote(x_rows(m, s), x_rows(m, s), c_send.at[which, t], c_recv.at[which, t], (d_sib, c))

    own.wait()
    for t in range(groups):
        if t > 0:
            s = (s_me - t + groups) % groups
            remote(tok_rows(s), x_rows(m_me, s), tok_send.at[t], tok_recv.at[t], class_peer(s)).wait_recv()
        z_copy(t).start()
        c_copy(0, t).start()
    for t in range(groups):
        z_arrival(t).wait_recv()
        c_copy(1, t).start()

    def multiply(m, d_from):
        rows = pl.ds(pl.multiple_of(m * slab, slab), slab)
        columns = pl.ds(pl.multiple_of(d_from * depth, depth), depth)
        return jnp.dot(x_ref[rows, columns], w_buf[d_from], preferred_element_type=jnp.float32)

    def acc_rows(m):
        return pl.ds(pl.multiple_of(m * slab, slab), slab)

    for copy in w_own:
        copy.wait()
    for t in range(dp):
        d_from = (d - t + dp) % dp
        if t > 0:
            for i, (src, dst) in enumerate(w_pieces(d, d_from)):
                remote(src, dst, w_send.at[t, i], w_recv.at[t, i], (d_from, c)).wait_recv()
        for m in (m_me, m_z):
            if t == 0:
                acc_ref[acc_rows(m), :] = multiply(m, d_from)
            else:
                acc_ref[acc_rows(m), :] += multiply(m, d_from)
    for which in range(2):
        for t in range(groups):
            c_arrival(which, t).wait_recv()
        m = (1 - dc) * 2 + (cz if which == 0 else 1 - cz)
        acc_ref[acc_rows(m), :] = multiply(m, 0)

        @pl.loop(1, dp)
        def _(k):
            acc_ref[acc_rows(m), :] += multiply(m, k)

    piece = chunk // ctx
    block = dp * ctx * piece

    def rows_of(i, q):
        src_d, src_c = i // ctx, i % ctx
        m = (src_d % 2) * 2 + src_c % 2
        s = (src_d // 2) * halves + src_c // 2
        start = pl.multiple_of(m * slab + s * chunk + q * piece, piece)
        return acc_ref[pl.ds(start, piece), :]

    @pl.loop(0, dp * ctx // 2)
    def _(pair):
        for q in range(ctx):
            both = jnp.concatenate([rows_of(pair * 2, q), rows_of(pair * 2 + 1, q)], axis=0)
            to = pl.multiple_of(q * block + pair * 2 * piece, 2 * piece)
            out_ref[pl.ds(to, 2 * piece), :] = both.astype(jnp.bfloat16)

    for t in range(groups):
        if t > 0:
            tok_copy(t).wait_send()
        z_copy(t).wait_send()
        c_copy(0, t).wait_send()
        c_copy(1, t).wait_send()
    for t in range(1, dp):
        for copy in w_copies(t):
            copy.wait_send()


def gathered_projection(outgoing, weights, dp, ctx):
    rows, width = outgoing.shape
    depth = weights.shape[0]
    groups = dp * ctx // 4
    chunk = rows // groups
    seq = 4 * groups * chunk
    dma = pltpu.SemaphoreType.DMA
    return pl.pallas_call(
        functools.partial(gather_kernel, dp, ctx, chunk),
        out_shape=jax.ShapeDtypeStruct((seq, PART_W), jnp.bfloat16),
        in_specs=[pl.BlockSpec(memory_space=pl.ANY)] * 2,
        out_specs=pl.BlockSpec(memory_space=pltpu.VMEM),
        scratch_shapes=[
            pltpu.VMEM((seq, width), jnp.bfloat16),
            pltpu.VMEM((dp, depth, PART_W), jnp.bfloat16),
            pltpu.VMEM((seq, PART_W), jnp.float32),
            dma, dma((3,)),
            dma((groups,)), dma((groups,)),
            dma((groups,)), dma((groups,)),
            dma((2, groups)), dma((2, groups)),
            dma((dp, 3)), dma((dp, 3)),
        ],
        compiler_params=pltpu.CompilerParams(
            collective_id=0, has_side_effects=True, vmem_limit_bytes=48 * 2**20
        ),
    )(outgoing, weights)


def on_device(dp, ctx, tokens, projection, placement, doc_lengths):
    row_count, width = tokens.shape
    dev_count = placement.shape[1]
    piece_rows = row_count // dev_count
    destinations = placement[0]
    slot_of = (
        jnp.zeros((dev_count,), jnp.int32)
        .at[destinations]
        .set(jnp.arange(dev_count, dtype=jnp.int32))
    )
    outgoing = tokens.reshape(dev_count, piece_rows, width)[slot_of]
    depth = projection.shape[0]
    direct = piece_rows == 8 and ctx == 4 and depth % 256 == 0
    d, c = lax.axis_index("dp"), lax.axis_index("ctx")
    seq_index = (d // 2) * 2 + c // 2
    if direct:
        projected = gathered_projection(outgoing.reshape(row_count, width), projection, dp, ctx)
        all_lengths = lax.all_gather(doc_lengths, "dp", axis=0, tiled=True)
        lengths = lax.dynamic_index_in_dim(all_lengths, seq_index, 0, keepdims=False)
    else:
        arrived = lax.all_to_all(outgoing, ("dp", "ctx"), split_axis=0, concat_axis=0, tiled=True)
        rows = lax.all_gather(arrived.reshape(row_count, width), "ctx", axis=0, tiled=True)
        cuts = [
            lax.dynamic_slice_in_dim(projection, base + c * w, w, axis=1)
            for base, w in ((0, Q_W), (HEADS * HEAD_DIM, HEAD_DIM), ((HEADS + KV_HEADS) * HEAD_DIM, HEAD_DIM))
        ]
        weights = lax.all_gather(jnp.concatenate(cuts, axis=1), "dp", axis=0, tiled=True)
        projected = jnp.dot(rows, weights, preferred_element_type=jnp.float32).astype(jnp.bfloat16)
        lengths = doc_lengths[0]
    mixed = attention(projected, lengths)
    by_source = jnp.transpose(mixed.reshape(ctx, dev_count, piece_rows, Q_W), (1, 0, 2, 3))
    returned = lax.all_to_all(by_source, ("dp", "ctx"), split_axis=0, concat_axis=0, tiled=True)
    if direct:
        parts = returned.reshape(dp // 2, 2, ctx // 2, 2, ctx, piece_rows, Q_W)
        parts = jnp.transpose(parts, (0, 2, 4, 5, 1, 3, 6))
    else:
        parts = returned.reshape(dp, ctx, ctx, piece_rows, Q_W)
        parts = jnp.transpose(parts, (0, 2, 3, 1, 4))
    blocks = parts.reshape(dev_count, piece_rows, HEADS * HEAD_DIM)
    return blocks[destinations].reshape(row_count, HEADS * HEAD_DIM)


def solution(mesh):
    return jax.shard_map(
        functools.partial(on_device, mesh.shape["dp"], mesh.shape["ctx"]),
        mesh=mesh,
        in_specs=(P(("dp", "ctx"), None), P("dp", None), P(("dp", "ctx"), None), P("dp", None)),
        out_specs=P(("dp", "ctx"), None),
        check_vma=False,
    )
```

time: 297 us -> 168 us (0.57)
  waiting for transfers between devices: 163 us -> 25 us
  Pallas kernels: 0 us -> 101 us
  blocking collectives: 54.9 us -> 10.3 us
  matrix products: 31.7 us -> 0 us
  between operations: 13.3 us -> 0.11 us
  starting transfers between devices: 2.99 us -> 15.5 us
  other arithmetic: 15.6 us -> 3.35 us
    all_gather x3 -> x0, waiting for transfers between devices: 137 us -> none  [the longest x1 89.7 us: on_device(): lax.all_gather(projection, 'dp', axis=0, tiled=True)]
    pallas_call x0 -> x2, Pallas kernels: none -> 101 us  [the longest x1 94.9 us: gathered_projection(): pl.pallas_call(functools.partial(gather_kernel, dp, ctx, chunk), out_shap...]
    all_to_all x1 -> x0, blocking collectives: 54.9 us -> none  [on_device(): lax.all_to_all(outgoing, ('dp', 'ctx'), split_axis=0, concat_axis=0, tile...]
    dot_general x9 -> x0, matrix products: 31.7 us -> none  [the longest x1 12.2 us: on_device(): jnp.dot(arrived, lax.all_gather(projection, 'dp', axis=0, tiled=True), pr...]
    all_to_all x1, starting transfers between devices: 2.91 us -> 15.5 us  [on_device(): lax.all_to_all(by_source, ('dp', 'ctx'), split_axis=0, concat_axis=0, til...]
    all_gather x0 -> x1, blocking collectives: none -> 10.3 us  [on_device(): all_lengths = lax.all_gather(doc_lengths, 'dp', axis=0, tiled=True)]
    reduce_sum x7 -> x0, other arithmetic: 5.12 us -> none  [the longest x4 4.87 us: per_head(): row_sum = row_sum * factor + jnp.sum(weights, axis=-1)]
  transfers between devices with their start and end apart: 4 -> 1, of which waited for: 4 -> 1; matrix products, arithmetic and copies ran while one was open for 5% -> 0% of each run, Pallas kernels for 0% -> 0%
where the time goes in v1:
time: 168 us; the launch traced here: 166 us
  Pallas kernels  101 us (60%)
  waiting for transfers between devices  25 us (15%)
  starting transfers between devices  15.5 us (9%)
  local copies, waits for them, and re-layouts  11.1 us (7%)
  blocking collectives  10.3 us (6%)
  other arithmetic  3.35 us (2%)
    pallas_call x1, Pallas kernels, gathered_projection(): pl.pallas_call(functools.partial(gather_kernel, dp, ctx, chunk), out_shap...  94.9 us
    all_to_all x1, waiting for transfers between devices, on_device(): lax.all_to_all(by_source, ('dp', 'ctx'), split_axis=0, concat_axis=0, til...  25 us
    all_to_all x1, starting transfers between devices, on_device(): lax.all_to_all(by_source, ('dp', 'ctx'), split_axis=0, concat_axis=0, til...  15.5 us
    all_gather x1, blocking collectives, on_device(): all_lengths = lax.all_gather(doc_lengths, 'dp', axis=0, tiled=True)  10.3 us
    pallas_call x1, Pallas kernels, attention(): pl.pallas_call(functools.partial(attention_kernel, 256), out_shape=jax.Sh...  5.84 us
  transfers between devices with their start and end apart: 1, of which 1 were waited for; matrix products, arithmetic and copies ran while one was open for 0% of the time, Pallas kernels for 0%

profile of v1, /device:TPU:0, one launch (start us, length us, event | category | flops | bytes accessed | tf_op | source)
XLA Modules:
  0.0 166.2 jit_solution(17809203796314517994)
XLA Ops:
  0.0 0.0 copy-start
  0.0 0.8 fusion.1
  0.8 0.7 scatter_custom_fusion
  1.5 10.3 %all-gather = s32[8,1,8]{2,1,0:T(1,128)S(1)} all-gather(s32[1,1,8]{2,1,0:T(1,128)} %bitcast.23), channel_id=1, replica_groups=mesh['dp'=8,'ctx'=4] {'dp'}, dimensions={0}, use_global_device_ids=true | all-gather | bytes 288 | tf_op jit(solution)/shard_map/all_gather | solution.py:293
  11.9 0.2 reduce-window.8
  12.0 0.1 select_reduce_fusion
  12.1 0.0 copy-done
  12.2 2.0 %gather_fusion = bf16[32,8,4096]{2,1,0:T(8,128)(2,1)} fusion(bf16[32,8,4096]{2,1,0:T(8,128)(2,1)S(1)} %bitcast.18, s32[1024]{0:T(1024)S(1)} %pad_clamp_fusion.1), kind=kCustom, calls=%fused_computation | custom fusion | bytes 4194432 | tf_op jit(solution)/shard_map/gather | solution.py:286
  14.2 0.0 copy-start.1
  14.2 1.6 copy-done.1
  15.8 94.9 %shard_map.46.proj_ref = bf16[1024,768]{1,0:T(8,128)(2,1)S(1)} custom-call(bf16[256,4096]{1,0:T(8,128)(2,1)S(1)} %bitcast.19, bf16[512,3072]{1,0:T(8,128)(2,1)} %w_ref.1), custom_call_target="tpu_custom_call" | custom-call | tf_op jit(solution)/shard_map/pallas_call | solution.py:255
  110.7 1.9 %fusion = (f32[1024,64]{1,0:T(8,128)S(1)}, f32[1024,64]{1,0:T(8,128)S(1)}, f32[1024,64]{1,0:T(8,128)S(1)}) fusion(f32[64]{0:T(128)S(1)} %multiply_power_fusion, f32[1024]{0:T(1024)S(1)} %subtract_convert_fusion), kind=kLoop, calls=%fused_computation.8 | loop fusion | flops 131072 | bytes 790784 | tf_op jit(solution)/shard_map/neg | solution.py:35
  112.6 0.3 pad_maximum_fusion
  113.0 0.2 broadcast_in_dim.16.begin_ref
  113.2 5.8 %shard_map.47 = bf16[1024,512]{1,0:T(8,128)(2,1)S(1)} custom-call(bf16[1024,768]{1,0:T(8,128)(2,1)S(1)} %shard_map.46.proj_ref, f32[1024,128]{1,0:T(8,128)S(1)} %get-tuple-element.8.cos_ref, f32[1024,128]{1,0:T(8,128)S(1)} %get-tuple-element.9.sin_ref, s32[1024,128]{1,0:T(8,128)S(1)} %broadcast_in_dim.16.begin_ref), custom_call_target="tpu_custom_call" | custom-call | tf_op jit(solution)/shard_map/pallas_call | solution.py:81
  119.0 1.1 copy.12
  120.1 15.5 %all-to-all-start = ((bf16[32,4,8,512]{3,2,1,0:T(8,128)(2,1)}), bf16[32,4,8,512]{3,2,1,0:T(8,128)(2,1)S(1)}, u32[]{:S(2)}, u32[]{:S(2)}) async-start(bf16[32,4,8,512]{3,2,1,0:T(8,128)(2,1)} %bitcast.22), calls=%async_computation | async-start | bytes 2097152 | tf_op jit(solution)/shard_map/all_to_all | solution.py:307
  135.7 25.0 %all-to-all-done = bf16[32,4,8,512]{3,2,1,0:T(8,128)(2,1)S(1)} async-done(((bf16[32,4,8,512]{3,2,1,0:T(8,128)(2,1)}), bf16[32,4,8,512]{3,2,1,0:T(8,128)(2,1)S(1)}, u32[]{:S(2)}, u32[]{:S(2)}) %all-to-all-start) | async-done | bytes 1048608 | tf_op jit(solution)/shard_map/all_to_all | solution.py:307
  160.7 2.1 %copy.10 = bf16[4,2,4,8,2,2,512]{6,5,4,3,2,1,0:T(2,128)(2,1)} copy(bf16[4,2,4,8,2,2,512]{6,3,2,5,1,4,0:T(8,128)(2,1)S(1)} %bitcast.21) | data formatting | bytes 2097152 | tf_op jit(solution)/shard_map/transpose | solution.py:310
  162.8 1.8 %reshape.89 = bf16[32,8,2048]{2,1,0:T(8,128)(2,1)S(1)} reshape(bf16[4,2,4,8,2,2,512]{6,5,4,3,2,1,0:T(2,128)(2,1)} %copy.10) | data formatting | bytes 2097152 | tf_op jit(solution)/shard_map/reshape | solution.py:314
  164.6 1.6 gather_fusion.1
  (7 shorter events, 0.0 us)
Async XLA Ops:
  0.0 12.1 %copy-start = (bf16[256,4096]{1,0:T(8,128)(2,1)S(1)}, bf16[256,4096]{1,0:T(8,128)(2,1)}, u32[]{:S(2)}) copy-start(bf16[256,4096]{1,0:T(8,128)(2,1)} %param.4) | copy-start | bytes 6291460
  14.2 1.6 copy-start.1
  120.1 40.6 %all-to-all-start = ((bf16[32,4,8,512]{3,2,1,0:T(8,128)(2,1)}), bf16[32,4,8,512]{3,2,1,0:T(8,128)(2,1)S(1)}, u32[]{:S(2)}, u32[]{:S(2)}) async-start(bf16[32,4,8,512]{3,2,1,0:T(8,128)(2,1)} %bitcast.22), calls=%async_computation | async-start | bytes 2097152 | tf_op jit(solution)/shard_map/all_to_all | solution.py:307

commit v2 on v1

v2 whole, which is shorter than its diff:
```python
import functools
import math

import jax
import jax.numpy as jnp
from jax import lax
from jax.experimental import pallas as pl
from jax.experimental.pallas import tpu as pltpu
from jax.sharding import PartitionSpec as P

HEAD_DIM = 128
HEADS = 16
KV_HEADS = 4
GROUP = HEADS // KV_HEADS
Q_W = GROUP * HEAD_DIM
PART_W = Q_W + 2 * HEAD_DIM
MOST = 512
MESH = pl.DeviceIdType.MESH

theta_base = 500000.0


def position_tables(lengths, seq):
    position = jnp.arange(seq, dtype=jnp.int32)
    ends = jnp.cumsum(lengths)
    begins = jnp.max(
        jnp.where(position[:, None] >= ends[None, :], ends[None, :], 0), axis=1
    )
    half = HEAD_DIM // 2
    frequency = theta_base ** (-2.0 * jnp.arange(half, dtype=jnp.float32) / HEAD_DIM)
    angles = (position - begins).astype(jnp.float32)[:, None] * frequency[None, :]
    cosine, sine = jnp.cos(angles), jnp.sin(angles)
    return (
        jnp.concatenate([cosine, cosine], axis=1),
        jnp.concatenate([-sine, sine], axis=1),
        jnp.broadcast_to(begins[:, None].astype(jnp.float32), (seq, HEAD_DIM)),
    )


def attention_kernel(block, proj_ref, cos_ref, sin_ref, begin_ref, out_ref, key_ref):
    seq = proj_ref.shape[0]
    factor = HEAD_DIM**-0.5 * math.log2(math.e)

    def rotated(rows, column):
        x = proj_ref[rows, column : column + HEAD_DIM].astype(jnp.float32)
        turned = pltpu.roll(x, HEAD_DIM // 2, 1)
        return (x * cos_ref[rows, :] + turned * sin_ref[rows, :]).astype(jnp.bfloat16)

    for b in range(seq // block):
        rows = slice(b * block, (b + 1) * block)
        key_ref[rows, :] = rotated(rows, Q_W)
    for b in range(seq // block):
        rows = slice(b * block, (b + 1) * block)
        first = max(0, (b * block - (MOST - 1)) // block * block)
        keys = slice(first, (b + 1) * block)
        width = (b + 1) * block - first
        at = first + lax.broadcasted_iota(jnp.int32, (block, width), 1)
        own = b * block + lax.broadcasted_iota(jnp.int32, (block, width), 0)
        allowed = (at.astype(jnp.float32) >= begin_ref[rows, 0:1]) & (at <= own)
        values = proj_ref[keys, Q_W + HEAD_DIM : PART_W]
        for h in range(GROUP):
            scores = lax.dot_general(
                rotated(rows, h * HEAD_DIM),
                key_ref[keys, :],
                (((1,), (1,)), ((), ())),
                preferred_element_type=jnp.float32,
            )
            scores = jnp.where(allowed, scores, -jnp.inf)
            top = jnp.max(scores, axis=1, keepdims=True)
            weights = jnp.exp2((scores - top) * factor)
            total = jnp.sum(weights, axis=1, keepdims=True)
            mixed = jnp.dot(
                weights.astype(jnp.bfloat16), values, preferred_element_type=jnp.float32
            )
            out_ref[rows, h * HEAD_DIM : (h + 1) * HEAD_DIM] = (mixed / total).astype(jnp.bfloat16)


def attention(projected, lengths):
    seq = projected.shape[0]
    cosine, sine, begins = position_tables(lengths, seq)
    return pl.pallas_call(
        functools.partial(attention_kernel, 256),
        out_shape=jax.ShapeDtypeStruct((seq, Q_W), jnp.bfloat16),
        in_specs=[pl.BlockSpec(memory_space=pltpu.VMEM)] * 4,
        out_specs=pl.BlockSpec(memory_space=pltpu.VMEM),
        scratch_shapes=[pltpu.VMEM((seq, HEAD_DIM), jnp.bfloat16)],
        compiler_params=pltpu.CompilerParams(vmem_limit_bytes=32 * 2**20),
    )(projected, cosine, sine, begins)


PHASES = (
    ((HEADS * HEAD_DIM, HEAD_DIM, 0, HEAD_DIM), ((HEADS + KV_HEADS) * HEAD_DIM, HEAD_DIM, HEAD_DIM, HEAD_DIM),
     (0, Q_W, 2 * HEAD_DIM, Q_W // 2)),
    ((Q_W // 2, Q_W, 2 * HEAD_DIM + Q_W // 2, Q_W // 2),),
)
PHASE_COLUMNS = ((0, 2 * HEAD_DIM + Q_W // 2), (2 * HEAD_DIM + Q_W // 2, Q_W // 2))
RET_W = Q_W // 2


def whole_kernel(dp, ctx, chunk, tok_ref, w_ref, tab_ref, ret_ref,
                 x_ref, w_buf, acc_ref, key_ref, val_ref, qry_ref, mix_ref, out_buf, tabs,
                 own_sem, wown_sem, tab_own, tab_send, tab_recv, tok_send, tok_recv, z_send, z_recv,
                 c_send, c_recv, w_send, w_recv, f_send, f_recv, r_own, r_send, r_recv):
    d, c = lax.axis_index("dp"), lax.axis_index("ctx")
    devices = dp * ctx
    me = d * ctx + c
    dc, cz = d % 2, c % 2
    groups = devices // 4
    halves = ctx // 2
    s_me = (d // 2) * halves + c // 2
    m_me = dc * 2 + cz
    m_z = dc * 2 + 1 - cz
    d_sib, c_sib = d + 1 - 2 * dc, c + 1 - 2 * cz
    slab = groups * chunk
    depth = w_ref.shape[0]
    piece = chunk // ctx
    block = devices * piece
    seq = ctx * block

    def class_peer(s):
        return ((s // halves) * 2 + dc, (s % halves) * 2 + cz)

    def remote(src, dst, send, recv, device):
        return pltpu.make_async_remote_copy(
            src_ref=src, dst_ref=dst, send_sem=send, recv_sem=recv, device_id=device, device_id_type=MESH
        )

    barrier = pltpu.get_barrier_semaphore()

    @pl.loop(1, devices)
    def _(t):
        other = (me + t) % devices
        pl.semaphore_signal(barrier, inc=1, device_id=(other // ctx, other % ctx), device_id_type=MESH)

    pl.semaphore_wait(barrier, devices - 1)

    def x_rows(m, s):
        return x_ref.at[pl.ds(pl.multiple_of(m * slab + s * chunk, chunk), chunk), :]

    def tok_rows(s):
        return tok_ref.at[pl.ds(pl.multiple_of(s * chunk, chunk), chunk), :]

    own = pltpu.make_async_copy(tok_rows(s_me), x_rows(m_me, s_me), own_sem)
    own.start()

    def tok_copy(t):
        s = (s_me + t) % groups
        return remote(tok_rows(s), x_rows(m_me, s_me), tok_send.at[t], tok_recv.at[t], class_peer(s))

    for t in range(1, groups):
        tok_copy(t).start()

    tab_mine = pltpu.make_async_copy(tab_ref, tabs.at[dc], tab_own)
    tab_mine.start()
    tab_out = remote(tab_ref, tabs.at[dc], tab_send, tab_recv, (d_sib, c))
    tab_out.start()
    tab_in = remote(tab_ref, tabs.at[1 - dc], tab_send, tab_recv, (d_sib, c))

    chip = d // 2
    chip_x = chip + 1 - 2 * (chip % 2)
    chip_y = (chip + 2) % 4
    chip_far = (chip_x + 2) % 4

    def w_parts(d_to, d_from, phase):
        g = (d_to % 2) * 2 + cz
        for i, (base, stride, to, width) in enumerate(PHASES[phase]):
            start = pl.multiple_of(base + g * stride, HEAD_DIM)
            yield (w_ref.at[:, pl.ds(start, width)], w_buf.at[d_from, :, to : to + width], 3 * phase + i)

    near = ((0, d_sib), (1, chip_x * 2 + dc), (2, chip_x * 2 + 1 - dc), (3, chip_y * 2 + dc), (4, chip_y * 2 + 1 - dc))

    def w_out(phase):
        return [remote(src, dst, w_send.at[slot, i], w_recv.at[slot, i], (d_to, c))
                for slot, d_to in near for src, dst, i in w_parts(d_to, d, phase)]

    def w_in(phase, slots):
        return [remote(src, dst, w_send.at[slot, i], w_recv.at[slot, i], (d_from, c))
                for slot, d_from in near if slot in slots for src, dst, i in w_parts(d, d_from, phase)]

    w_own = [pltpu.make_async_copy(src, dst, wown_sem.at[i])
             for phase in range(2) for src, dst, i in w_parts(d, d, phase)]

    half = depth // 2

    def f_parts(chip_from, way, phase, chip_to):
        for core in range(2):
            for i, (_, _, to, width) in enumerate(PHASES[phase]):
                there = w_buf.at[chip_from * 2 + core, way * half : (way + 1) * half, to : to + width]
                yield remote(there, there, f_send.at[way, core, 3 * phase + i], f_recv.at[way, core, 3 * phase + i],
                             (chip_to * 2 + dc, c))

    def f_out(phase, way):
        return list(f_parts((chip_x, chip_y)[way], way, phase, (chip_y, chip_x)[way]))

    def f_in(phase, way):
        return list(f_parts(chip_far, way, phase, (chip_y, chip_x)[way]))

    for copy in w_out(0):
        copy.start()
    for copy in w_own:
        copy.start()
    for copy in w_out(1):
        copy.start()

    def came(t):
        return (s_me - t + groups) % groups

    def z_copy(t):
        return remote(x_rows(m_me, came(t)), x_rows(m_me, came(t)), z_send.at[t], z_recv.at[t], (d, c_sib))

    def z_arrival(t):
        return remote(x_rows(m_z, came(t)), x_rows(m_z, came(t)), z_send.at[t], z_recv.at[t], (d, c_sib))

    def c_copy(which, t):
        at = x_rows(m_z if which else m_me, came(t))
        return remote(at, at, c_send.at[which, t], c_recv.at[which, t], (d_sib, c))

    def c_arrival(which, t):
        at = x_rows((1 - dc) * 2 + (1 - cz if which else cz), came(t))
        return remote(at, at, c_send.at[which, t], c_recv.at[which, t], (d_sib, c))

    own.wait()
    for t in range(groups):
        if t > 0:
            remote(tok_rows(came(t)), x_rows(m_me, came(t)), tok_send.at[t], tok_recv.at[t],
                   class_peer(came(t))).wait_recv()
        z_copy(t).start()
        c_copy(0, t).start()

    def forward_weights(phase):
        for way in range(2):
            for copy in w_in(phase, ((1, 2), (3, 4))[way]):
                copy.wait_recv()
            for copy in f_out(phase, way):
                copy.start()

    for t in range(groups):
        if t == groups // 2:
            forward_weights(0)
        z_arrival(t).wait_recv()
        c_copy(1, t).start()
    forward_weights(1)

    def multiply(m, phase):
        rows = pl.ds(pl.multiple_of(m * slab, slab), slab)
        first, width = PHASE_COLUMNS[phase]

        def product(k):
            columns = pl.ds(pl.multiple_of(k * depth, depth), depth)
            return jnp.dot(x_ref[rows, columns], w_buf[k, :, first : first + width],
                           preferred_element_type=jnp.float32)

        acc_ref[rows, 0:width] = product(0)

        @pl.loop(1, dp)
        def _(k):
            acc_ref[rows, 0:width] += product(k)

    def rows_of(i, q, first, width):
        src_d, src_c = i // ctx, i % ctx
        m = (src_d % 2) * 2 + src_c % 2
        s = (src_d // 2) * halves + src_c // 2
        start = pl.multiple_of(m * slab + s * chunk + q * piece, piece)
        return acc_ref[pl.ds(start, piece), first : first + width]

    seq_slot = c // 2

    def rotate(x, at):
        x = x.astype(jnp.bfloat16).astype(jnp.float32)
        turned = pltpu.roll(x, HEAD_DIM // 2, 1)
        cosine = tabs[seq_slot, pl.ds(at, 2 * piece), :]
        sine = tabs[seq_slot, pl.ds(pl.multiple_of(seq + at, 2 * piece), 2 * piece), :]
        return (x * cosine + turned * sine).astype(jnp.bfloat16)

    def pack(phase):
        @pl.loop(0, devices // 2)
        def _(pair):
            for q in range(ctx):
                def both(first):
                    return jnp.concatenate(
                        [rows_of(pair * 2 + i, q, first, HEAD_DIM) for i in range(2)], axis=0)

                at = pl.multiple_of(q * block + pair * 2 * piece, 2 * piece)
                to = pl.ds(at, 2 * piece)
                if phase == 0:
                    key_ref[to, :] = rotate(both(0), at)
                    val_ref[to, :] = both(HEAD_DIM).astype(jnp.bfloat16)
                base = 2 * HEAD_DIM if phase == 0 else 0
                for h in range(GROUP // 2):
                    qry_ref[to, h * HEAD_DIM : (h + 1) * HEAD_DIM] = rotate(both(base + h * HEAD_DIM), at)

    factor = HEAD_DIM**-0.5 * math.log2(math.e)

    def attend():
        for b in range(ctx):
            rows = slice(b * block, (b + 1) * block)
            first = max(0, (b * block - (MOST - 1)) // block * block)
            keys = slice(first, (b + 1) * block)
            width = (b + 1) * block - first
            at = first + lax.broadcasted_iota(jnp.int32, (block, width), 1)
            at_own = b * block + lax.broadcasted_iota(jnp.int32, (block, width), 0)
            begin = tabs[seq_slot, 2 * seq + b * block : 2 * seq + (b + 1) * block, 0:1]
            allowed = (at.astype(jnp.float32) >= begin) & (at <= at_own)
            for h in range(GROUP // 2):
                scores = lax.dot_general(
                    qry_ref[rows, h * HEAD_DIM : (h + 1) * HEAD_DIM], key_ref[keys, :],
                    (((1,), (1,)), ((), ())), preferred_element_type=jnp.float32,
                )
                scores = jnp.where(allowed, scores, -jnp.inf)
                top = jnp.max(scores, axis=1, keepdims=True)
                weights = jnp.exp2((scores - top) * factor)
                total = jnp.sum(weights, axis=1, keepdims=True)
                mixed = jnp.dot(weights.astype(jnp.bfloat16), val_ref[keys, :],
                                preferred_element_type=jnp.float32)
                mix_ref[rows, h * HEAD_DIM : (h + 1) * HEAD_DIM] = mixed / total

    def ret_at(s, m, phase):
        return ret_ref.at[pl.ds(pl.multiple_of(s * chunk, chunk), chunk),
                          pl.ds(pl.multiple_of(m * Q_W + phase * RET_W, RET_W), RET_W)]

    def buf_at(i, phase):
        return out_buf.at[phase, pl.ds(pl.multiple_of(i * chunk, chunk), chunk), :]

    def ret_copy(phase, t):
        i = (me + t) % devices
        return remote(buf_at(i, phase), ret_at(s_me, m_me, phase), r_send.at[phase, t], r_recv.at[phase, t],
                      (i // ctx, i % ctx))

    def ret_arrival(phase, t):
        i = (me - t + devices) % devices
        src_d, src_c = i // ctx, i % ctx
        s = (src_d // 2) * halves + src_c // 2
        m = (src_d % 2) * 2 + src_c % 2
        return remote(buf_at(i, phase), ret_at(s, m, phase), r_send.at[phase, t], r_recv.at[phase, t],
                      (src_d, src_c))

    def own_ret(phase):
        return pltpu.make_async_copy(buf_at(me, phase), ret_at(s_me, m_me, phase), r_own.at[phase])

    def send_back(phase):
        def ready(i):
            parts = [mix_ref[pl.ds(pl.multiple_of(q * block + i * piece, piece), piece), :] for q in range(ctx)]
            out_buf[phase, pl.ds(pl.multiple_of(i * chunk, chunk), chunk), :] = (
                jnp.concatenate(parts, axis=0).astype(jnp.bfloat16))

        @pl.loop(1, devices)
        def _(t):
            ready((me + t) % devices)
            ret_copy(phase, t).start()

        ready(me)
        own_ret(phase).start()

    tab_mine.wait()
    tab_in.wait_recv()
    for copy in w_own:
        copy.wait()
    for phase in range(2):
        for copy in w_in(phase, (0,)) + f_in(phase, 0) + f_in(phase, 1):
            copy.wait_recv()
        multiply(m_me, phase)
        multiply(m_z, phase)
        for which in range(2):
            if phase == 0:
                for t in range(groups):
                    c_arrival(which, t).wait_recv()
            multiply((1 - dc) * 2 + (1 - cz if which else cz), phase)
        pack(phase)
        attend()
        send_back(phase)

    tab_out.wait_send()
    for t in range(groups):
        if t > 0:
            tok_copy(t).wait_send()
        z_copy(t).wait_send()
        c_copy(0, t).wait_send()
        c_copy(1, t).wait_send()
    for phase in range(2):
        for copy in w_out(phase) + f_out(phase, 0) + f_out(phase, 1):
            copy.wait_send()
        own_ret(phase).wait()

        @pl.loop(1, devices)
        def _(t):
            ret_copy(phase, t).wait_send()
            ret_arrival(phase, t).wait_recv()


def attended_blocks(outgoing, weights, tables, dp, ctx):
    rows, width = outgoing.shape
    depth = weights.shape[0]
    devices = dp * ctx
    groups = devices // 4
    chunk = rows // groups
    seq = 4 * rows
    dma = pltpu.SemaphoreType.DMA
    return pl.pallas_call(
        functools.partial(whole_kernel, dp, ctx, chunk),
        out_shape=jax.ShapeDtypeStruct((rows, HEADS * HEAD_DIM), jnp.bfloat16),
        in_specs=[pl.BlockSpec(memory_space=pl.ANY)] * 3,
        out_specs=pl.BlockSpec(memory_space=pl.ANY),
        scratch_shapes=[
            pltpu.VMEM((seq, width), jnp.bfloat16),
            pltpu.VMEM((dp, depth, PART_W), jnp.bfloat16),
            pltpu.VMEM((seq, PHASE_COLUMNS[0][1]), jnp.float32),
            pltpu.VMEM((seq, HEAD_DIM), jnp.bfloat16),
            pltpu.VMEM((seq, HEAD_DIM), jnp.bfloat16),
            pltpu.VMEM((seq, RET_W), jnp.bfloat16),
            pltpu.VMEM((seq, RET_W), jnp.float32),
            pltpu.VMEM((2, seq, RET_W), jnp.bfloat16),
            pltpu.VMEM((2, 3 * seq, HEAD_DIM), jnp.float32),
            dma, dma((4,)), dma, dma, dma,
            dma((groups,)), dma((groups,)),
            dma((groups,)), dma((groups,)),
            dma((2, groups)), dma((2, groups)),
            dma((5, 4)), dma((5, 4)),
            dma((2, 2, 4)), dma((2, 2, 4)),
            dma((2,)), dma((2, devices)), dma((2, devices)),
        ],
        compiler_params=pltpu.CompilerParams(
            collective_id=0, has_side_effects=True, vmem_limit_bytes=48 * 2**20
        ),
    )(outgoing, weights, tables)


def on_device(dp, ctx, tokens, projection, placement, doc_lengths):
    row_count, width = tokens.shape
    dev_count = placement.shape[1]
    piece_rows = row_count // dev_count
    destinations = placement[0]
    slot_of = (
        jnp.zeros((dev_count,), jnp.int32)
        .at[destinations]
        .set(jnp.arange(dev_count, dtype=jnp.int32))
    )
    outgoing = tokens.reshape(dev_count, piece_rows, width)[slot_of]
    depth = projection.shape[0]
    if dp == 8 and ctx == 4 and piece_rows == 8:
        tables = jnp.concatenate(position_tables(doc_lengths[0], ctx * row_count), axis=0)
        blocks = attended_blocks(outgoing.reshape(row_count, width), projection, tables, dp, ctx)
    else:
        c = lax.axis_index("ctx")
        arrived = lax.all_to_all(outgoing, ("dp", "ctx"), split_axis=0, concat_axis=0, tiled=True)
        rows = lax.all_gather(arrived.reshape(row_count, width), "ctx", axis=0, tiled=True)
        cuts = [
            lax.dynamic_slice_in_dim(projection, base + c * w, w, axis=1)
            for base, w in ((0, Q_W), (HEADS * HEAD_DIM, HEAD_DIM), ((HEADS + KV_HEADS) * HEAD_DIM, HEAD_DIM))
        ]
        weights = lax.all_gather(jnp.concatenate(cuts, axis=1), "dp", axis=0, tiled=True)
        projected = jnp.dot(rows, weights, preferred_element_type=jnp.float32).astype(jnp.bfloat16)
        mixed = attention(projected, doc_lengths[0])
        by_source = jnp.transpose(mixed.reshape(ctx, dev_count, piece_rows, Q_W), (1, 0, 2, 3))
        returned = lax.all_to_all(by_source, ("dp", "ctx"), split_axis=0, concat_axis=0, tiled=True)
        parts = returned.reshape(dp, ctx, ctx, piece_rows, Q_W)
        blocks = jnp.transpose(parts, (0, 2, 3, 1, 4))
    blocks = blocks.reshape(dev_count, piece_rows, HEADS * HEAD_DIM)
    return blocks[destinations].reshape(row_count, HEADS * HEAD_DIM)


def solution(mesh):
    return jax.shard_map(
        functools.partial(on_device, mesh.shape["dp"], mesh.shape["ctx"]),
        mesh=mesh,
        in_specs=(P(("dp", "ctx"), None), P("dp", None), P(("dp", "ctx"), None), P("dp", None)),
        out_specs=P(("dp", "ctx"), None),
        check_vma=False,
    )
```

time: 168 us -> 134 us (0.80)
  waiting for transfers between devices: 25 us -> 0 us
  Pallas kernels: 101 us -> 121 us
  starting transfers between devices: 15.5 us -> 0 us
  blocking collectives: 10.3 us -> 0 us
  local copies, waits for them, and re-layouts: 11.1 us -> 7.48 us
    all_to_all x1 -> x0, waiting for transfers between devices: 25 us -> none  [on_device(): lax.all_to_all(by_source, ('dp', 'ctx'), split_axis=0, concat_axis=0, til...]
    pallas_call x2 -> x1, Pallas kernels: 101 us -> 121 us  [attended_blocks(): pl.pallas_call(functools.partial(whole_kernel, dp, ctx, chunk), out_shape...]
    all_to_all x1 -> x0, starting transfers between devices: 15.5 us -> none  [on_device(): lax.all_to_all(by_source, ('dp', 'ctx'), split_axis=0, concat_axis=0, til...]
    all_gather x1 -> x0, blocking collectives: 10.3 us -> none  [on_device(): all_lengths = lax.all_gather(doc_lengths, 'dp', axis=0, tiled=True)]
    reshape x2 -> x0, local copies, waits for them, and re-layouts: 2.94 us -> none  [the longest x1 1.82 us: on_device(): blocks = parts.reshape(dev_count, piece_rows, HEADS * HEAD_DIM)]
    transpose x1 -> x0, local copies, waits for them, and re-layouts: 2.05 us -> none  [on_device(): parts = jnp.transpose(parts, (0, 2, 4, 5, 1, 3, 6))]
    cos x0 -> x1, other arithmetic: none -> 1.9 us  [position_tables(): cosine, sine = (jnp.cos(angles), jnp.sin(angles))]
    neg x1 -> x0, other arithmetic: 1.9 us -> none  [position_tables(): -sine]
  transfers between devices with their start and end apart: 1 -> 0, of which waited for: 1 -> 0; matrix products, arithmetic and copies ran while one was open for 0% -> 0% of each run, Pallas kernels for 0% -> 0%
where the time goes in v2:
time: 134 us; the launch traced here: 133 us
  Pallas kernels  121 us (90%)
  local copies, waits for them, and re-layouts  7.48 us (6%)
  other arithmetic  4.9 us (4%)
    pallas_call x1, Pallas kernels, attended_blocks(): pl.pallas_call(functools.partial(whole_kernel, dp, ctx, chunk), out_shape...  121 us
    unnamed x8, local copies, waits for them, and re-layouts  3.01 us

profile of v2, /device:TPU:0, one launch (start us, length us, event | category | flops | bytes accessed | tf_op | source)
XLA Modules:
  0.0 133.5 jit_solution(6034852123343859168)
XLA Ops:
  0.0 0.0 copy-start
  0.0 1.0 reduce-window.8
  1.0 0.1 select_reduce_fusion
  1.1 1.9 %multiply_cosine_fusion = (f32[1024,64]{1,0:T(8,128)S(1)}, f32[1024,64]{1,0:T(8,128)S(1)}, f32[1024,64]{1,0:T(8,128)S(1)}) fusion(f32[64]{0:T(128)S(1)} %multiply_power_fusion, f32[1024]{0:T(1024)S(1)} %get-tuple-element.9), kind=kLoop, calls=%fused_computation.5 | loop fusion | flops 131072 | bytes 790784 | tf_op jit(solution)/shard_map/cos | solution.py:32
  3.0 0.0 copy-start.3
  3.0 1.9 %maximum_maximum_fusion.tab_ref = f32[3072,128]{1,0:T(8,128)} fusion(f32[1024,64]{1,0:T(8,128)S(1)} %get-tuple-element.7, f32[1024,64]{1,0:T(8,128)S(1)} %get-tuple-element.6, f32[1024,64]{1,0:T(8,128)S(1)} %get-tuple-element.5, f32[3072]{0:T(1024)S(1)} %pad.4.clone), kind=kLoop, calls=%fused_computation.3 | loop fusion | flops 1572864 | bytes 2371584 | tf_op jit(solution)/shard_map/concatenate | solution.py:440
  4.9 0.0 copy-done.3
  4.9 0.9 scatter_custom_fusion
  5.8 0.0 copy-done
  5.8 2.0 %gather_fusion = bf16[32,8,4096]{2,1,0:T(8,128)(2,1)} fusion(bf16[32,8,4096]{2,1,0:T(8,128)(2,1)S(1)} %bitcast.10, s32[1024]{0:T(1024)S(1)} %pad_clamp_fusion.1), kind=kCustom, calls=%fused_computation | custom fusion | bytes 4194432 | tf_op jit(solution)/shard_map/gather | solution.py:437
  7.9 0.0 copy-start.1
  7.9 1.6 %copy-done.1 = bf16[32,8,4096]{2,1,0:T(8,128)(2,1)S(1)} copy-done((bf16[32,8,4096]{2,1,0:T(8,128)(2,1)S(1)}, bf16[32,8,4096]{2,1,0:T(8,128)(2,1)}, u32[]{:S(2)}) %copy-start.1) | copy-done | bytes 2097176
  9.5 0.0 copy-start.2
  9.5 1.4 %copy-done.2 = f32[3072,128]{1,0:T(8,128)S(1)} copy-done((f32[3072,128]{1,0:T(8,128)S(1)}, f32[3072,128]{1,0:T(8,128)}, u32[]{:S(2)}) %copy-start.2) | copy-done | bytes 1572888
  10.9 121.0 %shard_map.46 = bf16[256,2048]{1,0:T(8,128)(2,1)S(1)} custom-call(bf16[256,4096]{1,0:T(8,128)(2,1)S(1)} %bitcast.11, bf16[512,3072]{1,0:T(8,128)(2,1)} %w_ref.1, f32[3072,128]{1,0:T(8,128)S(1)} %copy-done.2), custom_call_target="tpu_custom_call" | custom-call | tf_op jit(solution)/shard_map/pallas_call | solution.py:398
  131.9 1.6 %gather_fusion.1 = bf16[32,8,2048]{2,1,0:T(8,128)(2,1)} fusion(bf16[32,8,2048]{2,1,0:T(8,128)(2,1)S(1)} %bitcast.12, s32[1024]{0:T(1024)S(1)} %pad_clamp_fusion), kind=kCustom, calls=%fused_computation.1 | custom fusion | bytes 2097280 | tf_op jit(solution)/shard_map/gather | solution.py:458
  (8 shorter events, 0.0 us)
Async XLA Ops:
  0.0 5.8 %copy-start = (bf16[256,4096]{1,0:T(8,128)(2,1)S(1)}, bf16[256,4096]{1,0:T(8,128)(2,1)}, u32[]{:S(2)}) copy-start(bf16[256,4096]{1,0:T(8,128)(2,1)} %param.4) | copy-start | bytes 6291460
  3.0 1.9 %copy-start.3 = (s32[1,32]{1,0:T(1,128)S(1)}, s32[1,32]{1,0:T(1,128)}, u32[]{:S(2)}) copy-start(s32[1,32]{1,0:T(1,128)} %param.6) | copy-start | bytes 388
  7.9 1.6 %copy-start.1 = (bf16[32,8,4096]{2,1,0:T(8,128)(2,1)S(1)}, bf16[32,8,4096]{2,1,0:T(8,128)(2,1)}, u32[]{:S(2)}) copy-start(bf16[32,8,4096]{2,1,0:T(8,128)(2,1)} %gather_fusion) | copy-start | bytes 6291460
  9.5 1.4 %copy-start.2 = (f32[3072,128]{1,0:T(8,128)S(1)}, f32[3072,128]{1,0:T(8,128)}, u32[]{:S(2)}) copy-start(f32[3072,128]{1,0:T(8,128)} %maximum_maximum_fusion.tab_ref) | copy-start | bytes 4718596

commit v3 on v2

--- a/solution.py
+++ b/solution.py
@@ -97,9 +97,9 @@
 RET_W = Q_W // 2
 
 
-def whole_kernel(dp, ctx, chunk, tok_ref, w_ref, tab_ref, ret_ref,
-                 x_ref, w_buf, acc_ref, key_ref, val_ref, qry_ref, mix_ref, out_buf, tabs,
-                 own_sem, wown_sem, tab_own, tab_send, tab_recv, tok_send, tok_recv, z_send, z_recv,
+def whole_kernel(dp, ctx, chunk, slot_ref, len_ref, tok_ref, w_ref, ret_ref,
+                 stage, ends, x_ref, w_buf, acc_ref, key_ref, val_ref, qry_ref, mix_ref, out_buf, tabs,
+                 own_sem, wown_sem, tab_send, tab_recv, tok_send, tok_recv, z_send, z_recv,
                  c_send, c_recv, w_send, w_recv, f_send, f_recv, r_own, r_send, r_recv):
     d, c = lax.axis_index("dp"), lax.axis_index("ctx")
     devices = dp * ctx
@@ -132,29 +132,34 @@
         other = (me + t) % devices
         pl.semaphore_signal(barrier, inc=1, device_id=(other // ctx, other % ctx), device_id_type=MESH)
 
+    @pl.loop(0, devices // 2, unroll=4)
+    def _(pair):
+        both = [tok_ref[slot_ref[pair * 2 + i]] for i in range(2)]
+        stage[pl.ds(pl.multiple_of(pair * 2 * piece, 2 * piece), 2 * piece), :] = jnp.concatenate(both, axis=0)
+
+    document = lax.broadcasted_iota(jnp.int32, ends.shape[1:], 0)
+    end, table = jnp.int32(0), jnp.zeros(ends.shape[1:], jnp.int32)
+    for j in range(ends.shape[1]):
+        end = end + len_ref[0, j]
+        table = jnp.where(document == j, end, table)
+    ends[dc] = table
+
     pl.semaphore_wait(barrier, devices - 1)
 
     def x_rows(m, s):
         return x_ref.at[pl.ds(pl.multiple_of(m * slab + s * chunk, chunk), chunk), :]
 
     def tok_rows(s):
-        return tok_ref.at[pl.ds(pl.multiple_of(s * chunk, chunk), chunk), :]
+        return stage.at[pl.ds(pl.multiple_of(s * chunk, chunk), chunk), :]
 
     own = pltpu.make_async_copy(tok_rows(s_me), x_rows(m_me, s_me), own_sem)
-    own.start()
 
     def tok_copy(t):
         s = (s_me + t) % groups
         return remote(tok_rows(s), x_rows(m_me, s_me), tok_send.at[t], tok_recv.at[t], class_peer(s))
 
-    for t in range(1, groups):
-        tok_copy(t).start()
-
-    tab_mine = pltpu.make_async_copy(tab_ref, tabs.at[dc], tab_own)
-    tab_mine.start()
-    tab_out = remote(tab_ref, tabs.at[dc], tab_send, tab_recv, (d_sib, c))
-    tab_out.start()
-    tab_in = remote(tab_ref, tabs.at[1 - dc], tab_send, tab_recv, (d_sib, c))
+    tab_out = remote(ends.at[dc], ends.at[dc], tab_send, tab_recv, (d_sib, c))
+    tab_in = remote(ends.at[1 - dc], ends.at[1 - dc], tab_send, tab_recv, (d_sib, c))
 
     chip = d // 2
     chip_x = chip + 1 - 2 * (chip % 2)
@@ -169,9 +174,9 @@
 
     near = ((0, d_sib), (1, chip_x * 2 + dc), (2, chip_x * 2 + 1 - dc), (3, chip_y * 2 + dc), (4, chip_y * 2 + 1 - dc))
 
-    def w_out(phase):
+    def w_out(phase, slots=range(5)):
         return [remote(src, dst, w_send.at[slot, i], w_recv.at[slot, i], (d_to, c))
-                for slot, d_to in near for src, dst, i in w_parts(d_to, d, phase)]
+                for slot, d_to in near if slot in slots for src, dst, i in w_parts(d_to, d, phase)]
 
     def w_in(phase, slots):
         return [remote(src, dst, w_send.at[slot, i], w_recv.at[slot, i], (d_from, c))
@@ -195,37 +200,63 @@
     def f_in(phase, way):
         return list(f_parts(chip_far, way, phase, (chip_y, chip_x)[way]))
 
-    for copy in w_out(0):
-        copy.start()
-    for copy in w_own:
-        copy.start()
-    for copy in w_out(1):
-        copy.start()
-
     def came(t):
         return (s_me - t + groups) % groups
 
     def z_copy(t):
-        return remote(x_rows(m_me, came(t)), x_rows(m_me, came(t)), z_send.at[t], z_recv.at[t], (d, c_sib))
+        at = x_rows(m_me, came(t)) if t else tok_rows(s_me)
+        return remote(at, x_rows(m_me, came(t)), z_send.at[t], z_recv.at[t], (d, c_sib))
 
     def z_arrival(t):
         return remote(x_rows(m_z, came(t)), x_rows(m_z, came(t)), z_send.at[t], z_recv.at[t], (d, c_sib))
 
     def c_copy(which, t):
-        at = x_rows(m_z if which else m_me, came(t))
-        return remote(at, at, c_send.at[which, t], c_recv.at[which, t], (d_sib, c))
+        to = x_rows(m_z if which else m_me, came(t))
+        at = to if t or which else tok_rows(s_me)
+        return remote(at, to, c_send.at[which, t], c_recv.at[which, t], (d_sib, c))
 
     def c_arrival(which, t):
         at = x_rows((1 - dc) * 2 + (1 - cz if which else cz), came(t))
         return remote(at, at, c_send.at[which, t], c_recv.at[which, t], (d_sib, c))
 
-    own.wait()
-    for t in range(groups):
-        if t > 0:
-            remote(tok_rows(came(t)), x_rows(m_me, came(t)), tok_send.at[t], tok_recv.at[t],
-                   class_peer(came(t))).wait_recv()
+    z_copy(0).start()
+    for t in range(1, groups):
+        tok_copy(t).start()
+        for copy in w_out(0, (t,) if t < 5 else ()):
+            copy.start()
+    tab_out.start()
+    c_copy(0, 0).start()
+    for copy in w_out(0, (0,)):
+        copy.start()
+    own.start()
+    for copy in w_own:
+        copy.start()
+
+    tab_in.wait_recv()
+
+    @pl.loop(0, seq // 64)
+    def _(n):
+        rows = pl.ds(pl.multiple_of(n * 64, 64), 64)
+        position = n * 64 + lax.broadcasted_iota(jnp.int32, (64, HEAD_DIM), 0)
+        lane = lax.broadcasted_iota(jnp.int32, (1, HEAD_DIM), 1)
+        begin = jnp.zeros((64, HEAD_DIM), jnp.int32)
+        for j in range(ends.shape[1]):
+            end = ends[c // 2, j : j + 1, :]
+            begin = jnp.maximum(begin, jnp.where(position >= end, end, 0))
+        spread = (lane % (HEAD_DIM // 2)).astype(jnp.float32) * (-2.0 * math.log(theta_base) / HEAD_DIM)
+        angles = (position - begin).astype(jnp.float32) * jnp.exp(spread)
+        sine = jnp.sin(angles)
+        tabs[0, rows, :] = jnp.cos(angles)
+        tabs[1, rows, :] = jnp.where(lane < HEAD_DIM // 2, -sine, sine)
+        tabs[2, rows, :] = begin.astype(jnp.float32)
+
+    for t in range(1, groups):
+        remote(tok_rows(came(t)), x_rows(m_me, came(t)), tok_send.at[t], tok_recv.at[t],
+               class_peer(came(t))).wait_recv()
         z_copy(t).start()
         c_copy(0, t).start()
+    for copy in w_out(1):
+        copy.start()
 
     def forward_weights(phase):
         for way in range(2):
@@ -263,17 +294,15 @@
         start = pl.multiple_of(m * slab + s * chunk + q * piece, piece)
         return acc_ref[pl.ds(start, piece), first : first + width]
 
-    seq_slot = c // 2
-
     def rotate(x, at):
         x = x.astype(jnp.bfloat16).astype(jnp.float32)
         turned = pltpu.roll(x, HEAD_DIM // 2, 1)
-        cosine = tabs[seq_slot, pl.ds(at, 2 * piece), :]
-        sine = tabs[seq_slot, pl.ds(pl.multiple_of(seq + at, 2 * piece), 2 * piece), :]
+        cosine = tabs[0, pl.ds(at, 2 * piece), :]
+        sine = tabs[1, pl.ds(at, 2 * piece), :]
         return (x * cosine + turned * sine).astype(jnp.bfloat16)
 
     def pack(phase):
-        @pl.loop(0, devices // 2)
+        @pl.loop(0, devices // 2, unroll=2)
         def _(pair):
             for q in range(ctx):
                 def both(first):
@@ -299,7 +328,7 @@
             width = (b + 1) * block - first
             at = first + lax.broadcasted_iota(jnp.int32, (block, width), 1)
             at_own = b * block + lax.broadcasted_iota(jnp.int32, (block, width), 0)
-            begin = tabs[seq_slot, 2 * seq + b * block : 2 * seq + (b + 1) * block, 0:1]
+            begin = tabs[2, rows, 0:1]
             allowed = (at.astype(jnp.float32) >= begin) & (at <= at_own)
             for h in range(GROUP // 2):
                 scores = lax.dot_general(
@@ -351,8 +380,7 @@
         ready(me)
         own_ret(phase).start()
 
-    tab_mine.wait()
-    tab_in.wait_recv()
+    own.wait()
     for copy in w_own:
         copy.wait()
     for phase in range(2):
@@ -387,10 +415,10 @@
             ret_arrival(phase, t).wait_recv()
 
 
-def attended_blocks(outgoing, weights, tables, dp, ctx):
-    rows, width = outgoing.shape
+def attended_blocks(slot_of, lengths, tokens, weights, dp, ctx):
+    devices, piece, width = tokens.shape
+    rows = devices * piece
     depth = weights.shape[0]
-    devices = dp * ctx
     groups = devices // 4
     chunk = rows // groups
     seq = 4 * rows
@@ -398,9 +426,16 @@
     return pl.pallas_call(
         functools.partial(whole_kernel, dp, ctx, chunk),
         out_shape=jax.ShapeDtypeStruct((rows, HEADS * HEAD_DIM), jnp.bfloat16),
-        in_specs=[pl.BlockSpec(memory_space=pl.ANY)] * 3,
+        in_specs=[
+            pl.BlockSpec(memory_space=pltpu.SMEM),
+            pl.BlockSpec(memory_space=pltpu.SMEM),
+            pl.BlockSpec(memory_space=pltpu.VMEM),
+            pl.BlockSpec(memory_space=pl.ANY),
+        ],
         out_specs=pl.BlockSpec(memory_space=pl.ANY),
         scratch_shapes=[
+            pltpu.VMEM((rows, width), jnp.bfloat16),
+            pltpu.VMEM((2, lengths.shape[1], HEAD_DIM), jnp.int32),
             pltpu.VMEM((seq, width), jnp.bfloat16),
             pltpu.VMEM((dp, depth, PART_W), jnp.bfloat16),
             pltpu.VMEM((seq, PHASE_COLUMNS[0][1]), jnp.float32),
@@ -409,8 +444,8 @@
             pltpu.VMEM((seq, RET_W), jnp.bfloat16),
             pltpu.VMEM((seq, RET_W), jnp.float32),
             pltpu.VMEM((2, seq, RET_W), jnp.bfloat16),
-            pltpu.VMEM((2, 3 * seq, HEAD_DIM), jnp.float32),
-            dma, dma((4,)), dma, dma, dma,
+            pltpu.VMEM((3, seq, HEAD_DIM), jnp.float32),
+            dma, dma((4,)), dma, dma,
             dma((groups,)), dma((groups,)),
             dma((groups,)), dma((groups,)),
             dma((2, groups)), dma((2, groups)),
@@ -421,7 +456,7 @@
         compiler_params=pltpu.CompilerParams(
             collective_id=0, has_side_effects=True, vmem_limit_bytes=48 * 2**20
         ),
-    )(outgoing, weights, tables)
+    )(slot_of, lengths, tokens, weights)
 
 
 def on_device(dp, ctx, tokens, projection, placement, doc_lengths):
@@ -429,19 +464,14 @@
     dev_count = placement.shape[1]
     piece_rows = row_count // dev_count
     destinations = placement[0]
-    slot_of = (
-        jnp.zeros((dev_count,), jnp.int32)
-        .at[destinations]
-        .set(jnp.arange(dev_count, dtype=jnp.int32))
-    )
-    outgoing = tokens.reshape(dev_count, piece_rows, width)[slot_of]
-    depth = projection.shape[0]
+    index = jnp.arange(dev_count, dtype=jnp.int32)
+    slot_of = jnp.sum(jnp.where(destinations[None, :] == index[:, None], index[None, :], 0), axis=1)
+    pieces = tokens.reshape(dev_count, piece_rows, width)
     if dp == 8 and ctx == 4 and piece_rows == 8:
-        tables = jnp.concatenate(position_tables(doc_lengths[0], ctx * row_count), axis=0)
-        blocks = attended_blocks(outgoing.reshape(row_count, width), projection, tables, dp, ctx)
+        blocks = attended_blocks(slot_of, doc_lengths, pieces, projection, dp, ctx)
     else:
         c = lax.axis_index("ctx")
-        arrived = lax.all_to_all(outgoing, ("dp", "ctx"), split_axis=0, concat_axis=0, tiled=True)
+        arrived = lax.all_to_all(pieces[slot_of], ("dp", "ctx"), split_axis=0, concat_axis=0, tiled=True)
         rows = lax.all_gather(arrived.reshape(row_count, width), "ctx", axis=0, tiled=True)
         cuts = [
             lax.dynamic_slice_in_dim(projection, base + c * w, w, axis=1)

time: 134 us -> 132 us (0.985)
  Pallas kernels: 121 us -> 126 us
  local copies, waits for them, and re-layouts: 7.48 us -> 3.83 us
  other arithmetic: 4.9 us -> 1.44 us
    pallas_call x1, Pallas kernels: 121 us -> 126 us  [attended_blocks(): pl.pallas_call(functools.partial(whole_kernel, dp, ctx, chunk), out_shape...]
    gather x1 -> x0, local copies, waits for them, and re-layouts: 2.03 us -> none  [on_device(): outgoing = tokens.reshape(dev_count, piece_rows, width)[slot_of]]
    cos x1 -> x0, other arithmetic: 1.9 us -> none  [position_tables(): cosine, sine = (jnp.cos(angles), jnp.sin(angles))]
    concatenate x1 -> x0, other arithmetic: 1.89 us -> none  [on_device(): jnp.concatenate(position_tables(doc_lengths[0], ctx * row_count), axis=0)]
    unnamed x8 -> x4, local copies, waits for them, and re-layouts: 3.01 us -> 2.24 us
where the time goes in v3:
time: 132 us
  Pallas kernels  126 us (95%)
  local copies, waits for them, and re-layouts  3.83 us (3%)
  other arithmetic  1.44 us (1%)
    pallas_call x1, Pallas kernels, attended_blocks(): pl.pallas_call(functools.partial(whole_kernel, dp, ctx, chunk), out_shape...  126 us

profile of v3, /device:TPU:0, one launch (start us, length us, event | category | flops | bytes accessed | tf_op | source)
XLA Modules:
  0.0 131.7 jit_solution(15659419944133243467)
XLA Ops:
  0.0 0.8 select_reduce_fusion.slot_ref
  0.8 0.7 fusion
  1.4 0.0 copy-start
  1.4 1.6 %copy-done = bf16[256,4096]{1,0:T(8,128)(2,1)S(1)} copy-done((bf16[256,4096]{1,0:T(8,128)(2,1)S(1)}, bf16[256,4096]{1,0:T(8,128)(2,1)}, u32[]{:S(2)}) %copy-start) | copy-done | bytes 2097176
  3.0 0.0 copy-start.1
  3.0 0.7 copy-done.1
  3.7 126.4 %shard_map.46 = bf16[256,2048]{1,0:T(8,128)(2,1)S(1)} custom-call(s32[32]{0:T(128)S(1)} %select_reduce_fusion.slot_ref, s32[1,8]{1,0:T(1,128)S(1)} %copy-done.1, bf16[32,8,4096]{2,1,0:T(8,128)(2,1)S(1)} %bitcast.9, bf16[512,3072]{1,0:T(8,128)(2,1)} %w_ref.1), custom_call_target="tpu_custom_call" | custom-call | tf_op jit(solution)/shard_map/pallas_call | solution.py:426
  130.1 1.6 %gather_fusion = bf16[32,8,2048]{2,1,0:T(8,128)(2,1)} fusion(bf16[32,8,2048]{2,1,0:T(8,128)(2,1)S(1)} %bitcast.8, s32[1024]{0:T(1024)S(1)} %pad_clamp_fusion), kind=kCustom, calls=%fused_computation | custom fusion | bytes 2097280 | tf_op jit(solution)/shard_map/gather | solution.py:488
  (1 shorter events, 0.0 us)
Async XLA Ops:
  1.4 1.6 %copy-start = (bf16[256,4096]{1,0:T(8,128)(2,1)S(1)}, bf16[256,4096]{1,0:T(8,128)(2,1)}, u32[]{:S(2)}) copy-start(bf16[256,4096]{1,0:T(8,128)(2,1)} %param.4) | copy-start | bytes 6291460
  3.0 0.7 copy-start.1

commit v4 on v3

--- a/solution.py
+++ b/solution.py
@@ -93,13 +93,10 @@
      (0, Q_W, 2 * HEAD_DIM, Q_W // 2)),
     ((Q_W // 2, Q_W, 2 * HEAD_DIM + Q_W // 2, Q_W // 2),),
 )
-PHASE_COLUMNS = ((0, 2 * HEAD_DIM + Q_W // 2), (2 * HEAD_DIM + Q_W // 2, Q_W // 2))
-RET_W = Q_W // 2
-
-
-def whole_kernel(dp, ctx, chunk, slot_ref, len_ref, tok_ref, w_ref, ret_ref,
-                 stage, ends, x_ref, w_buf, acc_ref, key_ref, val_ref, qry_ref, mix_ref, out_buf, tabs,
-                 own_sem, wown_sem, tab_send, tab_recv, tok_send, tok_recv, z_send, z_recv,
+
+def whole_kernel(dp, ctx, chunk, slot_ref, len_ref, tok_hbm, w_ref, ret_ref,
+                 tok_ref, stage, ends, x_ref, w_buf, acc_ref, key_ref, val_ref, qry_ref, mix_ref, out_buf, tabs,
+                 in_sem, own_sem, wown_sem, tab_send, tab_recv, tok_send, tok_recv, z_send, z_recv,
                  c_send, c_recv, w_send, w_recv, f_send, f_recv, r_own, r_send, r_recv):
     d, c = lax.axis_index("dp"), lax.axis_index("ctx")
     devices = dp * ctx
@@ -111,11 +108,14 @@
     m_me = dc * 2 + cz
     m_z = dc * 2 + 1 - cz
     d_sib, c_sib = d + 1 - 2 * dc, c + 1 - 2 * cz
-    slab = groups * chunk
+    part = chunk // 2
+    slab = groups * part
     depth = w_ref.shape[0]
     piece = chunk // ctx
     block = devices * piece
     seq = ctx * block
+    rows_half = seq // 2
+    quarters = ctx // 2
 
     def class_peer(s):
         return ((s // halves) * 2 + dc, (s % halves) * 2 + cz)
@@ -125,17 +125,15 @@
             src_ref=src, dst_ref=dst, send_sem=send, recv_sem=recv, device_id=device, device_id_type=MESH
         )
 
+    tok_in = pltpu.make_async_copy(tok_hbm, tok_ref, in_sem)
+    tok_in.start()
+
     barrier = pltpu.get_barrier_semaphore()
 
     @pl.loop(1, devices)
     def _(t):
         other = (me + t) % devices
         pl.semaphore_signal(barrier, inc=1, device_id=(other // ctx, other % ctx), device_id_type=MESH)
-
-    @pl.loop(0, devices // 2, unroll=4)
-    def _(pair):
-        both = [tok_ref[slot_ref[pair * 2 + i]] for i in range(2)]
-        stage[pl.ds(pl.multiple_of(pair * 2 * piece, 2 * piece), 2 * piece), :] = jnp.concatenate(both, axis=0)
 
     document = lax.broadcasted_iota(jnp.int32, ends.shape[1:], 0)
     end, table = jnp.int32(0), jnp.zeros(ends.shape[1:], jnp.int32)
@@ -146,17 +144,24 @@
 
     pl.semaphore_wait(barrier, devices - 1)
 
-    def x_rows(m, s):
-        return x_ref.at[pl.ds(pl.multiple_of(m * slab + s * chunk, chunk), chunk), :]
-
-    def tok_rows(s):
-        return stage.at[pl.ds(pl.multiple_of(s * chunk, chunk), chunk), :]
-
-    own = pltpu.make_async_copy(tok_rows(s_me), x_rows(m_me, s_me), own_sem)
-
-    def tok_copy(t):
+    def gather(s, h):
+        at = s * ctx + h * quarters
+        rows = [tok_ref[slot_ref[at + q]] for q in range(quarters)]
+        start = pl.multiple_of(s * chunk + h * part, part)
+        stage[pl.ds(start, part), :] = jnp.concatenate(rows, axis=0)
+
+    def x_rows(m, s, h):
+        return x_ref.at[pl.ds(pl.multiple_of(h * rows_half + m * slab + s * part, part), part), :]
+
+    def tok_rows(s, h):
+        return stage.at[pl.ds(pl.multiple_of(s * chunk + h * part, part), part), :]
+
+    def own_copy(h):
+        return pltpu.make_async_copy(tok_rows(s_me, h), x_rows(m_me, s_me, h), own_sem.at[h])
+
+    def tok_copy(t, h):
         s = (s_me + t) % groups
-        return remote(tok_rows(s), x_rows(m_me, s_me), tok_send.at[t], tok_recv.at[t], class_peer(s))
+        return remote(tok_rows(s, h), x_rows(m_me, s_me, h), tok_send.at[h, t], tok_recv.at[h, t], class_peer(s))
 
     tab_out = remote(ends.at[dc], ends.at[dc], tab_send, tab_recv, (d_sib, c))
     tab_in = remote(ends.at[1 - dc], ends.at[1 - dc], tab_send, tab_recv, (d_sib, c))
@@ -203,34 +208,65 @@
     def came(t):
         return (s_me - t + groups) % groups
 
-    def z_copy(t):
-        at = x_rows(m_me, came(t)) if t else tok_rows(s_me)
-        return remote(at, x_rows(m_me, came(t)), z_send.at[t], z_recv.at[t], (d, c_sib))
-
-    def z_arrival(t):
-        return remote(x_rows(m_z, came(t)), x_rows(m_z, came(t)), z_send.at[t], z_recv.at[t], (d, c_sib))
-
-    def c_copy(which, t):
-        to = x_rows(m_z if which else m_me, came(t))
-        at = to if t or which else tok_rows(s_me)
-        return remote(at, to, c_send.at[which, t], c_recv.at[which, t], (d_sib, c))
-
-    def c_arrival(which, t):
-        at = x_rows((1 - dc) * 2 + (1 - cz if which else cz), came(t))
-        return remote(at, at, c_send.at[which, t], c_recv.at[which, t], (d_sib, c))
-
-    z_copy(0).start()
+    def tok_arrival(t, h):
+        return remote(tok_rows(came(t), h), x_rows(m_me, came(t), h), tok_send.at[h, t], tok_recv.at[h, t],
+                      class_peer(came(t)))
+
+    def z_copy(t, h):
+        to = x_rows(m_me, came(t), h)
+        at = to if t else tok_rows(s_me, h)
+        return remote(at, to, z_send.at[h, t], z_recv.at[h, t], (d, c_sib))
+
+    def z_arrival(t, h):
+        at = x_rows(m_z, came(t), h)
+        return remote(at, at, z_send.at[h, t], z_recv.at[h, t], (d, c_sib))
+
+    def c_copy(which, t, h):
+        to = x_rows(m_z if which else m_me, came(t), h)
+        at = to if t or which else tok_rows(s_me, h)
+        return remote(at, to, c_send.at[h, which, t], c_recv.at[h, which, t], (d_sib, c))
+
+    def c_arrival(which, t, h):
+        at = x_rows((1 - dc) * 2 + (1 - cz if which else cz), came(t), h)
+        return remote(at, at, c_send.at[h, which, t], c_recv.at[h, which, t], (d_sib, c))
+
+    def forward_class(h, ts):
+        for t in ts:
+            tok_arrival(t, h).wait_recv()
+            z_copy(t, h).start()
+            c_copy(0, t, h).start()
+
+    def forward_z(h, ts):
+        for t in ts:
+            z_arrival(t, h).wait_recv()
+            c_copy(1, t, h).start()
+
+    def start_own(h):
+        gather(s_me, h)
+        z_copy(0, h).start()
+        c_copy(0, 0, h).start()
+        own_copy(h).start()
+
+    tab_out.start()
+    tok_in.wait()
     for t in range(1, groups):
-        tok_copy(t).start()
+        gather((s_me + t) % groups, 0)
+        tok_copy(t, 0).start()
+        if t == 1:
+            start_own(0)
         for copy in w_out(0, (t,) if t < 5 else ()):
             copy.start()
-    tab_out.start()
-    c_copy(0, 0).start()
-    for copy in w_out(0, (0,)):
+    for copy in w_out(0, (0,)) + w_out(1):
         copy.start()
-    own.start()
     for copy in w_own:
         copy.start()
+
+    for t in range(1, groups):
+        gather((s_me + t) % groups, 1)
+    forward_class(0, range(1, groups))
+    for t in range(1, groups):
+        tok_copy(t, 1).start()
+    start_own(1)
 
     tab_in.wait_recv()
 
@@ -250,14 +286,6 @@
         tabs[1, rows, :] = jnp.where(lane < HEAD_DIM // 2, -sine, sine)
         tabs[2, rows, :] = begin.astype(jnp.float32)
 
-    for t in range(1, groups):
-        remote(tok_rows(came(t)), x_rows(m_me, came(t)), tok_send.at[t], tok_recv.at[t],
-               class_peer(came(t))).wait_recv()
-        z_copy(t).start()
-        c_copy(0, t).start()
-    for copy in w_out(1):
-        copy.start()
-
     def forward_weights(phase):
         for way in range(2):
             for copy in w_in(phase, ((1, 2), (3, 4))[way]):
@@ -265,34 +293,18 @@
             for copy in f_out(phase, way):
                 copy.start()
 
-    for t in range(groups):
-        if t == groups // 2:
-            forward_weights(0)
-        z_arrival(t).wait_recv()
-        c_copy(1, t).start()
+    forward_z(0, range(groups // 2))
+    forward_weights(0)
+    forward_z(0, range(groups // 2, groups))
+    forward_class(1, range(1, groups))
     forward_weights(1)
 
-    def multiply(m, phase):
-        rows = pl.ds(pl.multiple_of(m * slab, slab), slab)
-        first, width = PHASE_COLUMNS[phase]
-
-        def product(k):
-            columns = pl.ds(pl.multiple_of(k * depth, depth), depth)
-            return jnp.dot(x_ref[rows, columns], w_buf[k, :, first : first + width],
-                           preferred_element_type=jnp.float32)
-
-        acc_ref[rows, 0:width] = product(0)
-
-        @pl.loop(1, dp)
-        def _(k):
-            acc_ref[rows, 0:width] += product(k)
-
-    def rows_of(i, q, first, width):
+    def rows_of(i, q, first):
         src_d, src_c = i // ctx, i % ctx
         m = (src_d % 2) * 2 + src_c % 2
         s = (src_d // 2) * halves + src_c // 2
-        start = pl.multiple_of(m * slab + s * chunk + q * piece, piece)
-        return acc_ref[pl.ds(start, piece), first : first + width]
+        start = pl.multiple_of(m * slab + s * part + q * piece, piece)
+        return acc_ref[pl.ds(start, piece), first : first + HEAD_DIM]
 
     def rotate(x, at):
         x = x.astype(jnp.bfloat16).astype(jnp.float32)
@@ -301,28 +313,29 @@
         sine = tabs[1, pl.ds(at, 2 * piece), :]
         return (x * cosine + turned * sine).astype(jnp.bfloat16)
 
-    def pack(phase):
+    def pack(half_at):
         @pl.loop(0, devices // 2, unroll=2)
         def _(pair):
-            for q in range(ctx):
+            for q in range(quarters):
                 def both(first):
-                    return jnp.concatenate(
-                        [rows_of(pair * 2 + i, q, first, HEAD_DIM) for i in range(2)], axis=0)
-
-                at = pl.multiple_of(q * block + pair * 2 * piece, 2 * piece)
+                    return jnp.concatenate([rows_of(pair * 2 + i, q, first) for i in range(2)], axis=0)
+
+                near_at = pl.multiple_of(q * block + pair * 2 * piece, 2 * piece)
+                at = pl.multiple_of(half_at * rows_half + near_at, 2 * piece)
                 to = pl.ds(at, 2 * piece)
-                if phase == 0:
-                    key_ref[to, :] = rotate(both(0), at)
-                    val_ref[to, :] = both(HEAD_DIM).astype(jnp.bfloat16)
-                base = 2 * HEAD_DIM if phase == 0 else 0
-                for h in range(GROUP // 2):
-                    qry_ref[to, h * HEAD_DIM : (h + 1) * HEAD_DIM] = rotate(both(base + h * HEAD_DIM), at)
+                key_ref[to, :] = rotate(both(0), at)
+                val_ref[to, :] = both(HEAD_DIM).astype(jnp.bfloat16)
+                for h in range(GROUP):
+                    qry_ref[pl.ds(near_at, 2 * piece), h * HEAD_DIM : (h + 1) * HEAD_DIM] = rotate(
+                        both((2 + h) * HEAD_DIM), at)
 
     factor = HEAD_DIM**-0.5 * math.log2(math.e)
 
-    def attend():
-        for b in range(ctx):
+    def attend(half_at):
+        for j in range(quarters):
+            b = half_at * quarters + j
             rows = slice(b * block, (b + 1) * block)
+            near_rows = slice(j * block, (j + 1) * block)
             first = max(0, (b * block - (MOST - 1)) // block * block)
             keys = slice(first, (b + 1) * block)
             width = (b + 1) * block - first
@@ -330,9 +343,9 @@
             at_own = b * block + lax.broadcasted_iota(jnp.int32, (block, width), 0)
             begin = tabs[2, rows, 0:1]
             allowed = (at.astype(jnp.float32) >= begin) & (at <= at_own)
-            for h in range(GROUP // 2):
+            for h in range(GROUP):
                 scores = lax.dot_general(
-                    qry_ref[rows, h * HEAD_DIM : (h + 1) * HEAD_DIM], key_ref[keys, :],
+                    qry_ref[near_rows, h * HEAD_DIM : (h + 1) * HEAD_DIM], key_ref[keys, :],
                     (((1,), (1,)), ((), ())), preferred_element_type=jnp.float32,
                 )
                 scores = jnp.where(allowed, scores, -jnp.inf)
@@ -341,78 +354,107 @@
                 total = jnp.sum(weights, axis=1, keepdims=True)
                 mixed = jnp.dot(weights.astype(jnp.bfloat16), val_ref[keys, :],
                                 preferred_element_type=jnp.float32)
-                mix_ref[rows, h * HEAD_DIM : (h + 1) * HEAD_DIM] = mixed / total
-
-    def ret_at(s, m, phase):
-        return ret_ref.at[pl.ds(pl.multiple_of(s * chunk, chunk), chunk),
-                          pl.ds(pl.multiple_of(m * Q_W + phase * RET_W, RET_W), RET_W)]
-
-    def buf_at(i, phase):
-        return out_buf.at[phase, pl.ds(pl.multiple_of(i * chunk, chunk), chunk), :]
-
-    def ret_copy(phase, t):
+                mix_ref[near_rows, h * HEAD_DIM : (h + 1) * HEAD_DIM] = mixed / total
+
+    def ret_at(s, m, h):
+        return ret_ref.at[pl.ds(pl.multiple_of(s * chunk + h * part, part), part),
+                          pl.ds(pl.multiple_of(m * Q_W, Q_W), Q_W)]
+
+    def buf_at(i, h):
+        return out_buf.at[h, pl.ds(pl.multiple_of(i * part, part), part), :]
+
+    def ret_copy(h, t):
         i = (me + t) % devices
-        return remote(buf_at(i, phase), ret_at(s_me, m_me, phase), r_send.at[phase, t], r_recv.at[phase, t],
-                      (i // ctx, i % ctx))
-
-    def ret_arrival(phase, t):
+        return remote(buf_at(i, h), ret_at(s_me, m_me, h), r_send.at[h, t], r_recv.at[h, t], (i // ctx, i % ctx))
+
+    def ret_arrival(h, t):
         i = (me - t + devices) % devices
         src_d, src_c = i // ctx, i % ctx
         s = (src_d // 2) * halves + src_c // 2
         m = (src_d % 2) * 2 + src_c % 2
-        return remote(buf_at(i, phase), ret_at(s, m, phase), r_send.at[phase, t], r_recv.at[phase, t],
-                      (src_d, src_c))
-
-    def own_ret(phase):
-        return pltpu.make_async_copy(buf_at(me, phase), ret_at(s_me, m_me, phase), r_own.at[phase])
-
-    def send_back(phase):
+        return remote(buf_at(i, h), ret_at(s, m, h), r_send.at[h, t], r_recv.at[h, t], (src_d, src_c))
+
+    def own_ret(h):
+        return pltpu.make_async_copy(buf_at(me, h), ret_at(s_me, m_me, h), r_own.at[h])
+
+    def send_back(h):
         def ready(i):
-            parts = [mix_ref[pl.ds(pl.multiple_of(q * block + i * piece, piece), piece), :] for q in range(ctx)]
-            out_buf[phase, pl.ds(pl.multiple_of(i * chunk, chunk), chunk), :] = (
+            parts = [mix_ref[pl.ds(pl.multiple_of(q * block + i * piece, piece), piece), :] for q in range(quarters)]
+            out_buf[h, pl.ds(pl.multiple_of(i * part, part), part), :] = (
                 jnp.concatenate(parts, axis=0).astype(jnp.bfloat16))
 
         @pl.loop(1, devices)
         def _(t):
             ready((me + t) % devices)
-            ret_copy(phase, t).start()
+            ret_copy(h, t).start()
 
         ready(me)
-        own_ret(phase).start()
-
-    own.wait()
+        own_ret(h).start()
+
+    own_copy(0).wait()
+    for t in range(groups):
+        for which in range(2):
+            c_arrival(which, t, 0).wait_recv()
     for copy in w_own:
         copy.wait()
-    for phase in range(2):
-        for copy in w_in(phase, (0,)) + f_in(phase, 0) + f_in(phase, 1):
+
+    def multiply(rows, k, start, extent):
+        columns = pl.ds(pl.multiple_of(k * depth + start, extent), extent)
+        return jnp.dot(x_ref[rows, columns], w_buf[k, start : start + extent, :],
+                       preferred_element_type=jnp.float32)
+
+    early = pl.ds(0, rows_half)
+    acc_ref[...] = multiply(early, d, 0, depth)
+    for copy in w_in(0, (0,)) + w_in(1, (0,)):
+        copy.wait_recv()
+    for _, d_from in near:
+        acc_ref[...] += multiply(early, d_from, 0, depth)
+    for way in range(2):
+        for copy in f_in(0, way) + f_in(1, way):
             copy.wait_recv()
-        multiply(m_me, phase)
-        multiply(m_z, phase)
-        for which in range(2):
-            if phase == 0:
-                for t in range(groups):
-                    c_arrival(which, t).wait_recv()
-            multiply((1 - dc) * 2 + (1 - cz if which else cz), phase)
-        pack(phase)
-        attend()
-        send_back(phase)
+        for core in range(2):
+            acc_ref[...] += multiply(early, chip_far * 2 + core, way * half, half)
+    forward_z(1, range(groups // 2))
+    pack(0)
+    attend(0)
+    send_back(0)
+
+    forward_z(1, range(groups // 2, groups))
+    own_copy(1).wait()
+    for which in range(2):
+        if which:
+            for t in range(groups):
+                c_arrival(0, t, 1).wait_recv()
+                c_arrival(1, t, 1).wait_recv()
+        base = (1 - dc if which else dc) * 2 * slab
+        to = pl.ds(pl.multiple_of(base, 2 * slab), 2 * slab)
+        rows = pl.ds(pl.multiple_of(rows_half + base, 2 * slab), 2 * slab)
+        acc_ref[to, :] = multiply(rows, 0, 0, depth)
+
+        @pl.loop(1, dp)
+        def _(k):
+            acc_ref[to, :] += multiply(rows, k, 0, depth)
+
+    pack(1)
+    attend(1)
+    send_back(1)
 
     tab_out.wait_send()
-    for t in range(groups):
-        if t > 0:
-            tok_copy(t).wait_send()
-        z_copy(t).wait_send()
-        c_copy(0, t).wait_send()
-        c_copy(1, t).wait_send()
-    for phase in range(2):
-        for copy in w_out(phase) + f_out(phase, 0) + f_out(phase, 1):
-            copy.wait_send()
-        own_ret(phase).wait()
+    for copy in w_out(0) + w_out(1) + [copy for way in range(2) for phase in range(2) for copy in f_out(phase, way)]:
+        copy.wait_send()
+    for h in range(2):
+        for t in range(groups):
+            if t > 0:
+                tok_copy(t, h).wait_send()
+            z_copy(t, h).wait_send()
+            c_copy(0, t, h).wait_send()
+            c_copy(1, t, h).wait_send()
+        own_ret(h).wait()
 
         @pl.loop(1, devices)
         def _(t):
-            ret_copy(phase, t).wait_send()
-            ret_arrival(phase, t).wait_recv()
+            ret_copy(h, t).wait_send()
+            ret_arrival(h, t).wait_recv()
 
 
 def attended_blocks(slot_of, lengths, tokens, weights, dp, ctx):
@@ -429,26 +471,27 @@
         in_specs=[
             pl.BlockSpec(memory_space=pltpu.SMEM),
             pl.BlockSpec(memory_space=pltpu.SMEM),
-            pl.BlockSpec(memory_space=pltpu.VMEM),
+            pl.BlockSpec(memory_space=pl.ANY),
             pl.BlockSpec(memory_space=pl.ANY),
         ],
         out_specs=pl.BlockSpec(memory_space=pl.ANY),
         scratch_shapes=[
+            pltpu.VMEM((devices, piece, width), jnp.bfloat16),
             pltpu.VMEM((rows, width), jnp.bfloat16),
             pltpu.VMEM((2, lengths.shape[1], HEAD_DIM), jnp.int32),
             pltpu.VMEM((seq, width), jnp.bfloat16),
             pltpu.VMEM((dp, depth, PART_W), jnp.bfloat16),
-            pltpu.VMEM((seq, PHASE_COLUMNS[0][1]), jnp.float32),
+            pltpu.VMEM((seq // 2, PART_W), jnp.float32),
             pltpu.VMEM((seq, HEAD_DIM), jnp.bfloat16),
             pltpu.VMEM((seq, HEAD_DIM), jnp.bfloat16),
-            pltpu.VMEM((seq, RET_W), jnp.bfloat16),
-            pltpu.VMEM((seq, RET_W), jnp.float32),
-            pltpu.VMEM((2, seq, RET_W), jnp.bfloat16),
+            pltpu.VMEM((seq // 2, Q_W), jnp.bfloat16),
+            pltpu.VMEM((seq // 2, Q_W), jnp.float32),
+            pltpu.VMEM((2, rows * 2, Q_W), jnp.bfloat16),
             pltpu.VMEM((3, seq, HEAD_DIM), jnp.float32),
-            dma, dma((4,)), dma, dma,
-            dma((groups,)), dma((groups,)),
-            dma((groups,)), dma((groups,)),
+            dma, dma((2,)), dma((4,)), dma, dma,
             dma((2, groups)), dma((2, groups)),
+            dma((2, groups)), dma((2, groups)),
+            dma((2, 2, groups)), dma((2, 2, groups)),
             dma((5, 4)), dma((5, 4)),
             dma((2, 2, 4)), dma((2, 2, 4)),
             dma((2,)), dma((2, devices)), dma((2, devices)),

time: 132 us -> 122 us (0.924)
  Pallas kernels: 126 us -> 116 us
    pallas_call x1, Pallas kernels: 126 us -> 116 us  [attended_blocks(): pl.pallas_call(functools.partial(whole_kernel, dp, ctx, chunk), out_shape...]
where the time goes in v4:
time: 122 us; the launch traced here: 121 us
  Pallas kernels  116 us (95%)
  local copies, waits for them, and re-layouts  3.83 us (3%)
  other arithmetic  1.44 us (1%)
    pallas_call x1, Pallas kernels, attended_blocks(): pl.pallas_call(functools.partial(whole_kernel, dp, ctx, chunk), out_shape...  116 us

profile of v4, /device:TPU:0, one launch (start us, length us, event | category | flops | bytes accessed | tf_op | source)
XLA Modules:
  0.0 121.4 jit_solution(17886361832838801882)
XLA Ops:
  0.0 0.8 select_reduce_fusion.slot_ref
  0.8 0.7 fusion
  1.4 0.0 copy-start
  1.4 1.6 %copy-done = bf16[256,4096]{1,0:T(8,128)(2,1)S(1)} copy-done((bf16[256,4096]{1,0:T(8,128)(2,1)S(1)}, bf16[256,4096]{1,0:T(8,128)(2,1)}, u32[]{:S(2)}) %copy-start) | copy-done | bytes 2097176
  3.0 0.0 copy-start.1
  3.0 0.7 copy-done.1
  3.7 116.1 %shard_map.46 = bf16[256,2048]{1,0:T(8,128)(2,1)S(1)} custom-call(s32[32]{0:T(128)S(1)} %select_reduce_fusion.slot_ref, s32[1,8]{1,0:T(1,128)S(1)} %copy-done.1, bf16[32,8,4096]{2,1,0:T(8,128)(2,1)S(1)} %bitcast.9, bf16[512,3072]{1,0:T(8,128)(2,1)} %w_ref.1), custom_call_target="tpu_custom_call" | custom-call | tf_op jit(solution)/shard_map/pallas_call | solution.py:468
  119.8 1.6 %gather_fusion = bf16[32,8,2048]{2,1,0:T(8,128)(2,1)} fusion(bf16[32,8,2048]{2,1,0:T(8,128)(2,1)S(1)} %bitcast.8, s32[1024]{0:T(1024)S(1)} %pad_clamp_fusion), kind=kCustom, calls=%fused_computation | custom fusion | bytes 2097280 | tf_op jit(solution)/shard_map/gather | solution.py:531
  (1 shorter events, 0.0 us)
Async XLA Ops:
  1.4 1.6 %copy-start = (bf16[256,4096]{1,0:T(8,128)(2,1)S(1)}, bf16[256,4096]{1,0:T(8,128)(2,1)}, u32[]{:S(2)}) copy-start(bf16[256,4096]{1,0:T(8,128)(2,1)} %param.4) | copy-start | bytes 6291460
  3.0 0.7 copy-start.1

commit v5 on v4

--- a/solution.py
+++ b/solution.py
@@ -94,6 +94,11 @@
     ((Q_W // 2, Q_W, 2 * HEAD_DIM + Q_W // 2, Q_W // 2),),
 )
 
+PHASE_COLUMNS = ((0, 2 * HEAD_DIM + Q_W // 2), (2 * HEAD_DIM + Q_W // 2, Q_W // 2))
+PHASE_HEADS = (range(0, GROUP // 2), range(GROUP // 2, GROUP))
+RET_W = Q_W // 2
+
+
 def whole_kernel(dp, ctx, chunk, slot_ref, len_ref, tok_hbm, w_ref, ret_ref,
                  tok_ref, stage, ends, x_ref, w_buf, acc_ref, key_ref, val_ref, qry_ref, mix_ref, out_buf, tabs,
                  in_sem, own_sem, wown_sem, tab_send, tab_recv, tok_send, tok_recv, z_send, z_recv,
@@ -256,17 +261,17 @@
             start_own(0)
         for copy in w_out(0, (t,) if t < 5 else ()):
             copy.start()
-    for copy in w_out(0, (0,)) + w_out(1):
+    for copy in w_out(0, (0,)):
         copy.start()
     for copy in w_own:
         copy.start()
 
     for t in range(1, groups):
         gather((s_me + t) % groups, 1)
+    start_own(1)
     forward_class(0, range(1, groups))
     for t in range(1, groups):
         tok_copy(t, 1).start()
-    start_own(1)
 
     tab_in.wait_recv()
 
@@ -295,9 +300,10 @@
 
     forward_z(0, range(groups // 2))
     forward_weights(0)
+    for copy in w_out(1):
+        copy.start()
     forward_z(0, range(groups // 2, groups))
     forward_class(1, range(1, groups))
-    forward_weights(1)
 
     def rows_of(i, q, first):
         src_d, src_c = i // ctx, i % ctx
@@ -313,8 +319,8 @@
         sine = tabs[1, pl.ds(at, 2 * piece), :]
         return (x * cosine + turned * sine).astype(jnp.bfloat16)
 
-    def pack(half_at):
-        @pl.loop(0, devices // 2, unroll=2)
+    def pack(half_at, phase):
+        @pl.loop(0, devices // 2, unroll=4)
         def _(pair):
             for q in range(quarters):
                 def both(first):
@@ -323,15 +329,16 @@
                 near_at = pl.multiple_of(q * block + pair * 2 * piece, 2 * piece)
                 at = pl.multiple_of(half_at * rows_half + near_at, 2 * piece)
                 to = pl.ds(at, 2 * piece)
-                key_ref[to, :] = rotate(both(0), at)
-                val_ref[to, :] = both(HEAD_DIM).astype(jnp.bfloat16)
-                for h in range(GROUP):
+                if phase == 0:
+                    key_ref[to, :] = rotate(both(0), at)
+                    val_ref[to, :] = both(HEAD_DIM).astype(jnp.bfloat16)
+                for h in PHASE_HEADS[phase]:
                     qry_ref[pl.ds(near_at, 2 * piece), h * HEAD_DIM : (h + 1) * HEAD_DIM] = rotate(
                         both((2 + h) * HEAD_DIM), at)
 
     factor = HEAD_DIM**-0.5 * math.log2(math.e)
 
-    def attend(half_at):
+    def attend(half_at, phase):
         for j in range(quarters):
             b = half_at * quarters + j
             rows = slice(b * block, (b + 1) * block)
@@ -343,7 +350,7 @@
             at_own = b * block + lax.broadcasted_iota(jnp.int32, (block, width), 0)
             begin = tabs[2, rows, 0:1]
             allowed = (at.astype(jnp.float32) >= begin) & (at <= at_own)
-            for h in range(GROUP):
+            for h in PHASE_HEADS[phase]:
                 scores = lax.dot_general(
                     qry_ref[near_rows, h * HEAD_DIM : (h + 1) * HEAD_DIM], key_ref[keys, :],
                     (((1,), (1,)), ((), ())), preferred_element_type=jnp.float32,
@@ -356,40 +363,51 @@
                                 preferred_element_type=jnp.float32)
                 mix_ref[near_rows, h * HEAD_DIM : (h + 1) * HEAD_DIM] = mixed / total
 
-    def ret_at(s, m, h):
+    def ret_at(s, m, h, phase):
         return ret_ref.at[pl.ds(pl.multiple_of(s * chunk + h * part, part), part),
-                          pl.ds(pl.multiple_of(m * Q_W, Q_W), Q_W)]
-
-    def buf_at(i, h):
-        return out_buf.at[h, pl.ds(pl.multiple_of(i * part, part), part), :]
-
-    def ret_copy(h, t):
+                          pl.ds(pl.multiple_of(m * Q_W + phase * RET_W, RET_W), RET_W)]
+
+    def buf_at(i, h, phase):
+        return out_buf.at[h, phase, pl.ds(pl.multiple_of(i * part, part), part), :]
+
+    def ret_copy(h, phase, t):
         i = (me + t) % devices
-        return remote(buf_at(i, h), ret_at(s_me, m_me, h), r_send.at[h, t], r_recv.at[h, t], (i // ctx, i % ctx))
-
-    def ret_arrival(h, t):
+        return remote(buf_at(i, h, phase), ret_at(s_me, m_me, h, phase), r_send.at[h, phase, t],
+                      r_recv.at[h, phase, t], (i // ctx, i % ctx))
+
+    def ret_arrival(h, phase, t):
         i = (me - t + devices) % devices
         src_d, src_c = i // ctx, i % ctx
         s = (src_d // 2) * halves + src_c // 2
         m = (src_d % 2) * 2 + src_c % 2
-        return remote(buf_at(i, h), ret_at(s, m, h), r_send.at[h, t], r_recv.at[h, t], (src_d, src_c))
-
-    def own_ret(h):
-        return pltpu.make_async_copy(buf_at(me, h), ret_at(s_me, m_me, h), r_own.at[h])
-
-    def send_back(h):
+        return remote(buf_at(i, h, phase), ret_at(s, m, h, phase), r_send.at[h, phase, t],
+                      r_recv.at[h, phase, t], (src_d, src_c))
+
+    def own_ret(h, phase):
+        return pltpu.make_async_copy(buf_at(me, h, phase), ret_at(s_me, m_me, h, phase), r_own.at[h, phase])
+
+    def send_back(h, phase):
         def ready(i):
-            parts = [mix_ref[pl.ds(pl.multiple_of(q * block + i * piece, piece), piece), :] for q in range(quarters)]
-            out_buf[h, pl.ds(pl.multiple_of(i * part, part), part), :] = (
+            parts = [
+                mix_ref[pl.ds(pl.multiple_of(q * block + i * piece, piece), piece),
+                        phase * RET_W : (phase + 1) * RET_W]
+                for q in range(quarters)
+            ]
+            out_buf[h, phase, pl.ds(pl.multiple_of(i * part, part), part), :] = (
                 jnp.concatenate(parts, axis=0).astype(jnp.bfloat16))
 
         @pl.loop(1, devices)
         def _(t):
             ready((me + t) % devices)
-            ret_copy(h, t).start()
+            ret_copy(h, phase, t).start()
 
         ready(me)
-        own_ret(h).start()
+        own_ret(h, phase).start()
+
+    def finish(h, phase):
+        pack(h, phase)
+        attend(h, phase)
+        send_back(h, phase)
 
     own_copy(0).wait()
     for t in range(groups):
@@ -398,26 +416,38 @@
     for copy in w_own:
         copy.wait()
 
-    def multiply(rows, k, start, extent):
+    def multiply(rows, k, start, extent, phase):
         columns = pl.ds(pl.multiple_of(k * depth + start, extent), extent)
-        return jnp.dot(x_ref[rows, columns], w_buf[k, start : start + extent, :],
+        first, width = PHASE_COLUMNS[phase]
+        return jnp.dot(x_ref[rows, columns], w_buf[k, start : start + extent, first : first + width],
                        preferred_element_type=jnp.float32)
 
+    def place(phase):
+        first, width = PHASE_COLUMNS[phase]
+        return slice(first, first + width)
+
+    def whole(to, rows, phase):
+        acc_ref[to, place(phase)] = multiply(rows, 0, 0, depth, phase)
+
+        @pl.loop(1, dp)
+        def _(k):
+            acc_ref[to, place(phase)] += multiply(rows, k, 0, depth, phase)
+
     early = pl.ds(0, rows_half)
-    acc_ref[...] = multiply(early, d, 0, depth)
-    for copy in w_in(0, (0,)) + w_in(1, (0,)):
+    acc_ref[:, place(0)] = multiply(early, d, 0, depth, 0)
+    for copy in w_in(0, (0,)):
         copy.wait_recv()
     for _, d_from in near:
-        acc_ref[...] += multiply(early, d_from, 0, depth)
+        acc_ref[:, place(0)] += multiply(early, d_from, 0, depth, 0)
+    forward_z(1, range(groups // 4))
     for way in range(2):
-        for copy in f_in(0, way) + f_in(1, way):
+        for copy in f_in(0, way):
             copy.wait_recv()
         for core in range(2):
-            acc_ref[...] += multiply(early, chip_far * 2 + core, way * half, half)
-    forward_z(1, range(groups // 2))
-    pack(0)
-    attend(0)
-    send_back(0)
+            acc_ref[:, place(0)] += multiply(early, chip_far * 2 + core, way * half, half, 0)
+    forward_z(1, range(groups // 4, groups // 2))
+    forward_weights(1)
+    finish(0, 0)
 
     forward_z(1, range(groups // 2, groups))
     own_copy(1).wait()
@@ -427,17 +457,15 @@
                 c_arrival(0, t, 1).wait_recv()
                 c_arrival(1, t, 1).wait_recv()
         base = (1 - dc if which else dc) * 2 * slab
-        to = pl.ds(pl.multiple_of(base, 2 * slab), 2 * slab)
-        rows = pl.ds(pl.multiple_of(rows_half + base, 2 * slab), 2 * slab)
-        acc_ref[to, :] = multiply(rows, 0, 0, depth)
-
-        @pl.loop(1, dp)
-        def _(k):
-            acc_ref[to, :] += multiply(rows, k, 0, depth)
-
-    pack(1)
-    attend(1)
-    send_back(1)
+        whole(pl.ds(pl.multiple_of(base, 2 * slab), 2 * slab),
+              pl.ds(pl.multiple_of(rows_half + base, 2 * slab), 2 * slab), 0)
+    finish(1, 0)
+
+    for copy in w_in(1, (0,)) + f_in(1, 0) + f_in(1, 1):
+        copy.wait_recv()
+    for h in range(2):
+        whole(early, pl.ds(h * rows_half, rows_half), 1)
+        finish(h, 1)
 
     tab_out.wait_send()
     for copy in w_out(0) + w_out(1) + [copy for way in range(2) for phase in range(2) for copy in f_out(phase, way)]:
@@ -449,12 +477,13 @@
             z_copy(t, h).wait_send()
             c_copy(0, t, h).wait_send()
             c_copy(1, t, h).wait_send()
-        own_ret(h).wait()
-
-        @pl.loop(1, devices)
-        def _(t):
-            ret_copy(h, t).wait_send()
-            ret_arrival(h, t).wait_recv()
+        for phase in range(2):
+            own_ret(h, phase).wait()
+
+            @pl.loop(1, devices)
+            def _(t):
+                ret_copy(h, phase, t).wait_send()
+                ret_arrival(h, phase, t).wait_recv()
 
 
 def attended_blocks(slot_of, lengths, tokens, weights, dp, ctx):
@@ -471,8 +500,8 @@
         in_specs=[
             pl.BlockSpec(memory_space=pltpu.SMEM),
             pl.BlockSpec(memory_space=pltpu.SMEM),
-            pl.BlockSpec(memory_space=pl.ANY),
-            pl.BlockSpec(memory_space=pl.ANY),
+            pl.BlockSpec(memory_space=pltpu.HBM),
+            pl.BlockSpec(memory_space=pltpu.HBM),
         ],
         out_specs=pl.BlockSpec(memory_space=pl.ANY),
         scratch_shapes=[
@@ -486,7 +515,7 @@
             pltpu.VMEM((seq, HEAD_DIM), jnp.bfloat16),
             pltpu.VMEM((seq // 2, Q_W), jnp.bfloat16),
             pltpu.VMEM((seq // 2, Q_W), jnp.float32),
-            pltpu.VMEM((2, rows * 2, Q_W), jnp.bfloat16),
+            pltpu.VMEM((2, 2, rows * 2, RET_W), jnp.bfloat16),
             pltpu.VMEM((3, seq, HEAD_DIM), jnp.float32),
             dma, dma((2,)), dma((4,)), dma, dma,
             dma((2, groups)), dma((2, groups)),
@@ -494,7 +523,7 @@
             dma((2, 2, groups)), dma((2, 2, groups)),
             dma((5, 4)), dma((5, 4)),
             dma((2, 2, 4)), dma((2, 2, 4)),
-            dma((2,)), dma((2, devices)), dma((2, devices)),
+            dma((2, 2)), dma((2, 2, devices)), dma((2, 2, devices)),
         ],
         compiler_params=pltpu.CompilerParams(
             collective_id=0, has_side_effects=True, vmem_limit_bytes=48 * 2**20

time: 122 us -> 118 us (0.967)
  Pallas kernels: 116 us -> 113 us
    pallas_call x1, Pallas kernels: 116 us -> 113 us  [attended_blocks(): pl.pallas_call(functools.partial(whole_kernel, dp, ctx, chunk), out_shape...]
where the time goes in v5:
time: 118 us
  Pallas kernels  113 us (96%)
  local copies, waits for them, and re-layouts  3.83 us (3%)
  other arithmetic  1.44 us (1%)
    pallas_call x1, Pallas kernels, attended_blocks(): pl.pallas_call(functools.partial(whole_kernel, dp, ctx, chunk), out_shape...  113 us

profile of v5, /device:TPU:0, one launch (start us, length us, event | category | flops | bytes accessed | tf_op | source)
XLA Modules:
  0.0 118.2 jit_solution(4426771755066192501)
XLA Ops:
  0.0 0.8 select_reduce_fusion.slot_ref
  0.8 0.7 fusion
  1.4 0.0 copy-start
  1.4 1.6 %copy-done = bf16[256,4096]{1,0:T(8,128)(2,1)S(1)} copy-done((bf16[256,4096]{1,0:T(8,128)(2,1)S(1)}, bf16[256,4096]{1,0:T(8,128)(2,1)}, u32[]{:S(2)}) %copy-start) | copy-done | bytes 2097176
  3.0 0.0 copy-start.1
  3.0 0.7 copy-done.1
  3.7 112.9 %shard_map.46 = bf16[256,2048]{1,0:T(8,128)(2,1)S(1)} custom-call(s32[32]{0:T(128)S(1)} %select_reduce_fusion.slot_ref, s32[1,8]{1,0:T(1,128)S(1)} %copy-done.1, bf16[32,8,4096]{2,1,0:T(8,128)(2,1)S(1)} %bitcast.9, bf16[512,3072]{1,0:T(8,128)(2,1)} %w_ref.1), custom_call_target="tpu_custom_call" | custom-call | tf_op jit(solution)/shard_map/pallas_call | solution.py:497
  116.6 1.6 %gather_fusion = bf16[32,8,2048]{2,1,0:T(8,128)(2,1)} fusion(bf16[32,8,2048]{2,1,0:T(8,128)(2,1)S(1)} %bitcast.8, s32[1024]{0:T(1024)S(1)} %pad_clamp_fusion), kind=kCustom, calls=%fused_computation | custom fusion | bytes 2097280 | tf_op jit(solution)/shard_map/gather | solution.py:560
  (1 shorter events, 0.0 us)
Async XLA Ops:
  1.4 1.6 %copy-start = (bf16[256,4096]{1,0:T(8,128)(2,1)S(1)}, bf16[256,4096]{1,0:T(8,128)(2,1)}, u32[]{:S(2)}) copy-start(bf16[256,4096]{1,0:T(8,128)(2,1)} %param.4) | copy-start | bytes 6291460
  3.0 0.7 copy-start.1

commit v6 on v5

--- a/solution.py
+++ b/solution.py
@@ -259,19 +259,18 @@
         tok_copy(t, 0).start()
         if t == 1:
             start_own(0)
-        for copy in w_out(0, (t,) if t < 5 else ()):
-            copy.start()
-    for copy in w_out(0, (0,)):
+    for t in range(1, groups):
+        gather((s_me + t) % groups, 1)
+        tok_copy(t, 1).start()
+        if t == 1:
+            start_own(1)
+    forward_class(0, range(1, groups // 2))
+    for copy in w_out(0, (1, 3, 2, 4, 0)):
         copy.start()
     for copy in w_own:
         copy.start()
 
-    for t in range(1, groups):
-        gather((s_me + t) % groups, 1)
-    start_own(1)
-    forward_class(0, range(1, groups))
-    for t in range(1, groups):
-        tok_copy(t, 1).start()
+    forward_class(0, range(groups // 2, groups))
 
     tab_in.wait_recv()
 
@@ -305,11 +304,11 @@
     forward_z(0, range(groups // 2, groups))
     forward_class(1, range(1, groups))
 
-    def rows_of(i, q, first):
+    def rows_of(h, i, q, first):
         src_d, src_c = i // ctx, i % ctx
         m = (src_d % 2) * 2 + src_c % 2
         s = (src_d // 2) * halves + src_c // 2
-        start = pl.multiple_of(m * slab + s * part + q * piece, piece)
+        start = pl.multiple_of(h * rows_half + m * slab + s * part + q * piece, piece)
         return acc_ref[pl.ds(start, piece), first : first + HEAD_DIM]
 
     def rotate(x, at):
@@ -324,7 +323,7 @@
         def _(pair):
             for q in range(quarters):
                 def both(first):
-                    return jnp.concatenate([rows_of(pair * 2 + i, q, first) for i in range(2)], axis=0)
+                    return jnp.concatenate([rows_of(half_at, pair * 2 + i, q, first) for i in range(2)], axis=0)
 
                 near_at = pl.multiple_of(q * block + pair * 2 * piece, 2 * piece)
                 at = pl.multiple_of(half_at * rows_half + near_at, 2 * piece)
@@ -426,25 +425,25 @@
         first, width = PHASE_COLUMNS[phase]
         return slice(first, first + width)
 
-    def whole(to, rows, phase):
-        acc_ref[to, place(phase)] = multiply(rows, 0, 0, depth, phase)
+    def whole(rows, phase):
+        acc_ref[rows, place(phase)] = multiply(rows, 0, 0, depth, phase)
 
         @pl.loop(1, dp)
         def _(k):
-            acc_ref[to, place(phase)] += multiply(rows, k, 0, depth, phase)
+            acc_ref[rows, place(phase)] += multiply(rows, k, 0, depth, phase)
 
     early = pl.ds(0, rows_half)
-    acc_ref[:, place(0)] = multiply(early, d, 0, depth, 0)
+    acc_ref[early, place(0)] = multiply(early, d, 0, depth, 0)
     for copy in w_in(0, (0,)):
         copy.wait_recv()
     for _, d_from in near:
-        acc_ref[:, place(0)] += multiply(early, d_from, 0, depth, 0)
+        acc_ref[early, place(0)] += multiply(early, d_from, 0, depth, 0)
     forward_z(1, range(groups // 4))
     for way in range(2):
         for copy in f_in(0, way):
             copy.wait_recv()
         for core in range(2):
-            acc_ref[:, place(0)] += multiply(early, chip_far * 2 + core, way * half, half, 0)
+            acc_ref[early, place(0)] += multiply(early, chip_far * 2 + core, way * half, half, 0)
     forward_z(1, range(groups // 4, groups // 2))
     forward_weights(1)
     finish(0, 0)
@@ -457,14 +456,22 @@
                 c_arrival(0, t, 1).wait_recv()
                 c_arrival(1, t, 1).wait_recv()
         base = (1 - dc if which else dc) * 2 * slab
-        whole(pl.ds(pl.multiple_of(base, 2 * slab), 2 * slab),
-              pl.ds(pl.multiple_of(rows_half + base, 2 * slab), 2 * slab), 0)
+        whole(pl.ds(pl.multiple_of(rows_half + base, 2 * slab), 2 * slab), 0)
     finish(1, 0)
 
-    for copy in w_in(1, (0,)) + f_in(1, 0) + f_in(1, 1):
+    for copy in w_in(1, (0,)):
         copy.wait_recv()
     for h in range(2):
-        whole(early, pl.ds(h * rows_half, rows_half), 1)
+        rows = pl.ds(h * rows_half, rows_half)
+        acc_ref[rows, place(1)] = multiply(rows, d, 0, depth, 1)
+        for _, d_from in near:
+            acc_ref[rows, place(1)] += multiply(rows, d_from, 0, depth, 1)
+    for copy in f_in(1, 0) + f_in(1, 1):
+        copy.wait_recv()
+    for h in range(2):
+        rows = pl.ds(h * rows_half, rows_half)
+        for core in range(2):
+            acc_ref[rows, place(1)] += multiply(rows, chip_far * 2 + core, 0, depth, 1)
         finish(h, 1)
 
     tab_out.wait_send()
@@ -510,7 +517,7 @@
             pltpu.VMEM((2, lengths.shape[1], HEAD_DIM), jnp.int32),
             pltpu.VMEM((seq, width), jnp.bfloat16),
             pltpu.VMEM((dp, depth, PART_W), jnp.bfloat16),
-            pltpu.VMEM((seq // 2, PART_W), jnp.float32),
+            pltpu.VMEM((seq, PART_W), jnp.float32),
             pltpu.VMEM((seq, HEAD_DIM), jnp.bfloat16),
             pltpu.VMEM((seq, HEAD_DIM), jnp.bfloat16),
             pltpu.VMEM((seq // 2, Q_W), jnp.bfloat16),
@@ -526,7 +533,7 @@
             dma((2, 2)), dma((2, 2, devices)), dma((2, 2, devices)),
         ],
         compiler_params=pltpu.CompilerParams(
-            collective_id=0, has_side_effects=True, vmem_limit_bytes=48 * 2**20
+            collective_id=0, has_side_effects=True, vmem_limit_bytes=62 * 2**20
         ),
     )(slot_of, lengths, tokens, weights)
 

time: 118 us -> 125 us (1.059)
  Pallas kernels: 113 us -> 120 us
    pallas_call x1, Pallas kernels: 113 us -> 120 us  [attended_blocks(): pl.pallas_call(functools.partial(whole_kernel, dp, ctx, chunk), out_shape...]
    unnamed x4 -> x0, local copies, waits for them, and re-layouts: 2.24 us -> none
where the time goes in v6:
time: 125 us
  Pallas kernels  120 us (96%)
  local copies, waits for them, and re-layouts  2.81 us (2%)
  other arithmetic  1.95 us (2%)
    pallas_call x1, Pallas kernels, attended_blocks(): pl.pallas_call(functools.partial(whole_kernel, dp, ctx, chunk), out_shape...  120 us
    gather x1, local copies, waits for them, and re-layouts, on_device(): return blocks[destinations].reshape(row_count, HEADS * HEAD_DIM)  2.81 us

profile of v6, /device:TPU:0, one launch (start us, length us, event | category | flops | bytes accessed | tf_op | source)
XLA Modules:
  0.0 125.2 jit_solution(16861178719402394776)
XLA Ops:
  0.0 1.3 %select_reduce_fusion.slot_ref = s32[32]{0:T(128)} fusion(s32[32]{0:T(128)} %bitcast.10), kind=kLoop, calls=%fused_computation.1 | loop fusion | flops 3040 | bytes 256 | tf_op jit(solution)/shard_map/reduce_sum | solution.py:547
  1.3 0.7 fusion
  1.9 120.4 %shard_map.46 = bf16[256,2048]{1,0:T(8,128)(2,1)} custom-call(s32[32]{0:T(128)} %select_reduce_fusion.slot_ref, s32[1,8]{1,0:T(1,128)} %len_ref.1, bf16[32,8,4096]{2,1,0:T(8,128)(2,1)} %bitcast.9, bf16[512,3072]{1,0:T(8,128)(2,1)} %w_ref.1), custom_call_target="tpu_custom_call" | custom-call | tf_op jit(solution)/shard_map/pallas_call | solution.py:504
  122.4 2.8 %gather_fusion = bf16[32,8,2048]{2,1,0:T(8,128)(2,1)} fusion(bf16[32,8,2048]{2,1,0:T(8,128)(2,1)} %bitcast.8, s32[1024]{0:T(1024)S(1)} %pad_clamp_fusion), kind=kCustom, calls=%fused_computation | custom fusion | bytes 2097280 | tf_op jit(solution)/shard_map/gather | solution.py:567
  (1 shorter events, 0.0 us)

commit v7 on v6

--- a/solution.py
+++ b/solution.py
@@ -252,6 +252,8 @@
         c_copy(0, 0, h).start()
         own_copy(h).start()
 
+    for copy in w_out(0, (1, 3, 2, 4)):
+        copy.start()
     tab_out.start()
     tok_in.wait()
     for t in range(1, groups):
@@ -259,18 +261,20 @@
         tok_copy(t, 0).start()
         if t == 1:
             start_own(0)
-    for t in range(1, groups):
-        gather((s_me + t) % groups, 1)
-        tok_copy(t, 1).start()
-        if t == 1:
-            start_own(1)
-    forward_class(0, range(1, groups // 2))
-    for copy in w_out(0, (1, 3, 2, 4, 0)):
+    for copy in w_out(0, (0,)):
         copy.start()
     for copy in w_own:
         copy.start()
+    for t in range(1, groups):
+        gather((s_me + t) % groups, 1)
+    start_own(1)
+    forward_class(0, range(1, groups // 2))
 
     forward_class(0, range(groups // 2, groups))
+    for t in range(1, groups):
+        tok_copy(t, 1).start()
+    for copy in w_out(1):
+        copy.start()
 
     tab_in.wait_recv()
 
@@ -297,11 +301,9 @@
             for copy in f_out(phase, way):
                 copy.start()
 
-    forward_z(0, range(groups // 2))
+    forward_z(0, range(2))
     forward_weights(0)
-    for copy in w_out(1):
-        copy.start()
-    forward_z(0, range(groups // 2, groups))
+    forward_z(0, range(2, groups))
     forward_class(1, range(1, groups))
 
     def rows_of(h, i, q, first):
@@ -439,13 +441,13 @@
     for _, d_from in near:
         acc_ref[early, place(0)] += multiply(early, d_from, 0, depth, 0)
     forward_z(1, range(groups // 4))
+    forward_weights(1)
     for way in range(2):
         for copy in f_in(0, way):
             copy.wait_recv()
         for core in range(2):
             acc_ref[early, place(0)] += multiply(early, chip_far * 2 + core, way * half, half, 0)
     forward_z(1, range(groups // 4, groups // 2))
-    forward_weights(1)
     finish(0, 0)
 
     forward_z(1, range(groups // 2, groups))

time: 125 us -> 127 us (1.016)
  Pallas kernels: 120 us -> 122 us
    pallas_call x1, Pallas kernels: 120 us -> 122 us  [attended_blocks(): pl.pallas_call(functools.partial(whole_kernel, dp, ctx, chunk), out_shape...]
where the time goes in v7:
time: 127 us
  Pallas kernels  122 us (96%)
  local copies, waits for them, and re-layouts  2.81 us (2%)
  other arithmetic  1.95 us (2%)
    pallas_call x1, Pallas kernels, attended_blocks(): pl.pallas_call(functools.partial(whole_kernel, dp, ctx, chunk), out_shape...  122 us
    gather x1, local copies, waits for them, and re-layouts, on_device(): return blocks[destinations].reshape(row_count, HEADS * HEAD_DIM)  2.81 us

profile of v7, /device:TPU:0, one launch (start us, length us, event | category | flops | bytes accessed | tf_op | source)
XLA Modules:
  0.0 127.2 jit_solution(16964667425679446866)
XLA Ops:
  0.0 1.3 %select_reduce_fusion.slot_ref = s32[32]{0:T(128)} fusion(s32[32]{0:T(128)} %bitcast.10), kind=kLoop, calls=%fused_computation.1 | loop fusion | flops 3040 | bytes 256 | tf_op jit(solution)/shard_map/reduce_sum | solution.py:549
  1.3 0.7 fusion
  1.9 122.4 %shard_map.46 = bf16[256,2048]{1,0:T(8,128)(2,1)} custom-call(s32[32]{0:T(128)} %select_reduce_fusion.slot_ref, s32[1,8]{1,0:T(1,128)} %len_ref.1, bf16[32,8,4096]{2,1,0:T(8,128)(2,1)} %bitcast.9, bf16[512,3072]{1,0:T(8,128)(2,1)} %w_ref.1), custom_call_target="tpu_custom_call" | custom-call | tf_op jit(solution)/shard_map/pallas_call | solution.py:506
  124.4 2.8 %gather_fusion = bf16[32,8,2048]{2,1,0:T(8,128)(2,1)} fusion(bf16[32,8,2048]{2,1,0:T(8,128)(2,1)} %bitcast.8, s32[1024]{0:T(1024)S(1)} %pad_clamp_fusion), kind=kCustom, calls=%fused_computation | custom fusion | bytes 2097280 | tf_op jit(solution)/shard_map/gather | solution.py:569
  (1 shorter events, 0.0 us)

commit v8 on v6

--- a/solution.py
+++ b/solution.py
@@ -533,7 +533,7 @@
             dma((2, 2)), dma((2, 2, devices)), dma((2, 2, devices)),
         ],
         compiler_params=pltpu.CompilerParams(
-            collective_id=0, has_side_effects=True, vmem_limit_bytes=62 * 2**20
+            collective_id=0, has_side_effects=True, vmem_limit_bytes=48 * 2**20
         ),
     )(slot_of, lengths, tokens, weights)
 

time: 125 us -> 126 us (level)
    unnamed x0 -> x4, local copies, waits for them, and re-layouts: none -> 2.24 us
where the time goes in v8:
time: 126 us
  Pallas kernels  120 us (95%)
  local copies, waits for them, and re-layouts  3.83 us (3%)
  other arithmetic  1.44 us (1%)
    pallas_call x1, Pallas kernels, attended_blocks(): pl.pallas_call(functools.partial(whole_kernel, dp, ctx, chunk), out_shape...  120 us

profile of v8, /device:TPU:0, one launch (start us, length us, event | category | flops | bytes accessed | tf_op | source)
XLA Modules:
  0.0 125.6 jit_solution(10076268657606962650)
XLA Ops:
  0.0 0.8 select_reduce_fusion.slot_ref
  0.8 0.7 fusion
  1.4 0.0 copy-start
  1.4 1.6 %copy-done = bf16[256,4096]{1,0:T(8,128)(2,1)S(1)} copy-done((bf16[256,4096]{1,0:T(8,128)(2,1)S(1)}, bf16[256,4096]{1,0:T(8,128)(2,1)}, u32[]{:S(2)}) %copy-start) | copy-done | bytes 2097176
  3.0 0.0 copy-start.1
  3.0 0.7 copy-done.1
  3.7 120.4 %shard_map.46 = bf16[256,2048]{1,0:T(8,128)(2,1)S(1)} custom-call(s32[32]{0:T(128)S(1)} %select_reduce_fusion.slot_ref, s32[1,8]{1,0:T(1,128)S(1)} %copy-done.1, bf16[32,8,4096]{2,1,0:T(8,128)(2,1)S(1)} %bitcast.9, bf16[512,3072]{1,0:T(8,128)(2,1)} %w_ref.1), custom_call_target="tpu_custom_call" | custom-call | tf_op jit(solution)/shard_map/pallas_call | solution.py:504
  124.1 1.6 %gather_fusion = bf16[32,8,2048]{2,1,0:T(8,128)(2,1)} fusion(bf16[32,8,2048]{2,1,0:T(8,128)(2,1)S(1)} %bitcast.8, s32[1024]{0:T(1024)S(1)} %pad_clamp_fusion), kind=kCustom, calls=%fused_computation | custom fusion | bytes 2097280 | tf_op jit(solution)/shard_map/gather | solution.py:567
  (1 shorter events, 0.0 us)
Async XLA Ops:
  1.4 1.6 %copy-start = (bf16[256,4096]{1,0:T(8,128)(2,1)S(1)}, bf16[256,4096]{1,0:T(8,128)(2,1)}, u32[]{:S(2)}) copy-start(bf16[256,4096]{1,0:T(8,128)(2,1)} %param.4) | copy-start | bytes 6291460
  3.0 0.7 copy-start.1
